TPU v7x, 128 devices: a whole 4x4x4 slice. The times are simulated.
128 devices in a mesh: dom: 128 (over x, y, z, core).
Axes of the slice: x: 4, y: 4, z: 4, core: 2. Of those that a mesh axis runs over, the one named last changes fastest.
Arguments:
- state: float32 [5, 125, 32768], P(None, None, 'dom'), may hold values from -6 to 6
- adjoint: float32 [5, 125, 32768], P(None, None, 'dom'), may hold values from -6 to 6
- order: int32 [32768], P('dom'), may hold values from 2 to 4
- neighbours: int32 [6, 32768], P(None, 'dom'), may hold values from -1 to 32767, as said below
- owner: int32 [32768, 1], P('dom'), may hold values from 0 to 127; in each aligned block of 256 rows (0 to 255, 256 to 511, ...) at most 4 rows name the same one
- jacobian: float32 [5, 5, 32768], P(None, None, 'dom'), may hold values from -6 to 6
- enrich: float32 [3, 216, 125], replicated, may hold values from -0.5 to 0.5
- volume: float32 [216, 125], replicated, may hold values from -0.5 to 0.5
Outputs:
- indicator: float32 [32768], P('dom')
- moved_state: float32 [5, 125, 65536], P(None, None, 'dom')
- moved_adjoint: float32 [5, 216, 65536], P(None, None, 'dom')
- slot_ids: int32 [65536], P('dom')
- slot_orders: int32 [65536], P('dom')
Inputs may be any that keep to these rules, and one draw needn't show every extreme that they name: Faces 0 and 1 join elements along the first mode direction, 2 and 3 along the second, 4 and 5 along the third, with equal orientation of the two other directions; if neighbours[f, e] = g >= 0 then neighbours[f XOR 1, g] = e. Every neighbour across faces 2 to 5 lies on the element's own device; across faces 0 and 1 it lies either on the element's own device or among the last 128 elements of the previous device or the first 128 of the next. Among the elements of one device at most 4 have the same new owner, and some owner gets exactly 4 of them.
All inputs are finite; a program needn't handle non-finite values.
Results may differ from a plain program's by a relative error of at most 0.0003.
Values sent between devices are 32-bit elements; how exact they have to be, the bound alone decides.
No kernel may reach another device: no remote copies, remote signals or barrier semaphores. Data moves between devices by JAX's collectives and lax.ppermute only.
A program may use at most 64 MiB of HBM per device.

v0:
```python
import jax
import jax.numpy as jnp
from jax import lax
from jax.sharding import PartitionSpec as P

NR = 8
NA = 16


precise = lax.Precision.HIGHEST


def extended_2(block, sides, width):
    for axis, dim in sides:
        count = lax.axis_size(axis)
        forward = [(i, i + 1) for i in range(count - 1)]
        backward = [(target, source) for source, target in forward]
        low = lax.ppermute(
            lax.slice_in_dim(block, block.shape[dim] - width, None, axis=dim), axis, forward
        )
        high = lax.ppermute(lax.slice_in_dim(block, 0, width, axis=dim), axis, backward)
        block = jnp.concatenate([low, block, high], axis=dim)
    return block


def mode_tables():
    small_modes = jnp.arange(125, dtype=jnp.int32)
    small_coords = jnp.stack([small_modes // 25, small_modes // 5 % 5, small_modes % 5])
    rich_modes = jnp.arange(216, dtype=jnp.int32)
    rich_coords = jnp.stack([rich_modes // 36, rich_modes // 6 % 6, rich_modes % 6])
    order_levels = jnp.arange(3, dtype=jnp.int32)[:, None] + 2
    keep_in = (jnp.max(small_coords, axis=0)[None, :] <= order_levels).astype(jnp.float32)
    keep_new = (jnp.max(rich_coords, axis=0)[None, :] == order_levels + 1).astype(jnp.float32)
    face_modes = jnp.arange(25, dtype=jnp.int32)
    trace_rows = []
    lift_rows = []
    for face_index in range(6):
        normal_axis = face_index // 2
        tangent_axes = [entry for entry in range(3) if entry != normal_axis]
        normal_index = small_coords[normal_axis]
        tangent_index = small_coords[tangent_axes[0]] * 5 + small_coords[tangent_axes[1]]
        rich_normal = rich_coords[normal_axis]
        rich_tangent = rich_coords[tangent_axes[0]] * 5 + rich_coords[tangent_axes[1]]
        in_range = (rich_coords[tangent_axes[0]] < 5) & (rich_coords[tangent_axes[1]] < 5)
        if face_index % 2 == 0:
            parity = jnp.where(normal_index % 2 == 1, -1.0, 1.0).astype(jnp.float32)
            rich_parity = jnp.where(rich_normal % 2 == 1, -1.0, 1.0).astype(jnp.float32)
        else:
            parity = jnp.ones((125,), jnp.float32)
            rich_parity = jnp.ones((216,), jnp.float32)
        trace_rows.append(
            (face_modes[:, None] == tangent_index[None, :]).astype(jnp.float32) * parity[None, :]
        )
        lift_weight = rich_parity * (2 * rich_normal + 1).astype(jnp.float32) * 0.5
        matches = (rich_tangent[:, None] == face_modes[None, :]) & in_range[:, None]
        lift_rows.append(matches.astype(jnp.float32) * lift_weight[:, None])
    return (keep_in, keep_new, jnp.stack(trace_rows), jnp.stack(lift_rows))


def enrich_adjoint(coarse, choose, keep_new, enrich):
    field_count = coarse.shape[0]
    column_count = coarse.shape[2]
    as_cube = coarse.reshape(field_count, 5, 5, 5, column_count)
    embedded = jnp.pad(as_cube, ((0, 0), (0, 1), (0, 1), (0, 1), (0, 0))).reshape(
        field_count, 216, column_count
    )
    new_modes = jnp.zeros((field_count, 216, column_count), jnp.float32)
    for degree in range(3):
        partial_term = jnp.einsum("nm,cme->cne", enrich[degree], coarse, precision=precise)
        new_modes = (
            new_modes + partial_term * (keep_new[degree][:, None] * choose[degree][None, :])[None]
        )
    return (embedded, new_modes)


def residual_of(coarse_state, traces, neighbour_traces, jacobian, volume, lift_table):
    jump_term = neighbour_traces - traces
    face_flux = jnp.zeros_like(jump_term)
    weighted = jnp.zeros_like(coarse_state)
    for field_index in range(jacobian.shape[0]):
        face_flux = (
            face_flux
            + jacobian[:, field_index][None, :, None, :] * jump_term[:, field_index][:, None, :, :]
        )
        weighted = weighted + jacobian[:, field_index][:, None, :] * coarse_state[field_index][None]
    residual = jnp.einsum("nm,cme->cne", volume, weighted, precision=precise)
    residual = residual + jnp.einsum("fnq,fcqe->cne", lift_table, face_flux, precision=precise)
    return residual


def select_columns(values, selector):
    leading = values.shape[:-1]
    flat = values.reshape(-1, values.shape[-1])
    picked = jnp.dot(flat, selector, precision=precise, preferred_element_type=jnp.float32)
    return picked.reshape(leading + (selector.shape[1],))


def body(state, adjoint, order, neighbours, owner, jacobian, enrich, volume):
    element_count = state.shape[2]
    device_count = lax.axis_size("dom")
    device_index = lax.axis_index("dom")
    margin = NR * NA
    keep_in, keep_new, trace_table, lift_table = mode_tables()
    choose = (order[None, :] - 2 == jnp.arange(3, dtype=jnp.int32)[:, None]).astype(jnp.float32)
    keep_mask = jnp.sum(choose[:, None, :] * keep_in[:, :, None], axis=0)
    coarse_state = state * keep_mask[None]
    coarse_adjoint = adjoint * keep_mask[None]
    extended = extended_2(coarse_state, (("dom", 2),), margin)
    traces = jnp.einsum("fqm,cme->fcqe", trace_table, extended, precision=precise)
    own_traces = traces[:, :, :, margin : margin + element_count]
    full_width = element_count + 2 * margin
    local_index = neighbours - (device_index * element_count - margin)
    positions = jnp.arange(full_width, dtype=jnp.int32)
    gathered = []
    for face_index in range(6):
        hits = (positions[:, None] == local_index[face_index][None, :]) & (
            neighbours[face_index] >= 0
        )[None, :]
        gathered.append(select_columns(traces[face_index ^ 1], hits.astype(jnp.float32)))
    neighbour_traces = jnp.stack(gathered)
    embedded, new_modes = enrich_adjoint(coarse_adjoint, choose, keep_new, enrich)
    residual = residual_of(coarse_state, own_traces, neighbour_traces, jacobian, volume, lift_table)
    indicator = jnp.abs(jnp.sum(new_modes * residual, axis=(0, 1))) * (1.0 / 216.0)
    targets = owner[:, 0]
    capacity = max(2, (2 * element_count + device_count - 1) // device_count)
    owner_hits = (targets[None, :] == jnp.arange(device_count, dtype=jnp.int32)[:, None]).astype(
        jnp.int32
    )
    arrival_rank = jnp.sum((jnp.cumsum(owner_hits, axis=1) - 1) * owner_hits, axis=0)
    slot_index = targets * capacity + arrival_rank
    slot_count = device_count * capacity
    slot_hits = slot_index[:, None] == jnp.arange(slot_count, dtype=jnp.int32)[None, :]
    slot_table = slot_hits.astype(jnp.float32)
    slot_ints = slot_hits.astype(jnp.int32)
    present = jnp.sum(slot_ints, axis=0) > 0
    local_ids = jnp.sum(slot_ints * jnp.arange(element_count, dtype=jnp.int32)[:, None], axis=0)
    element_ids = jnp.where(present, device_index * element_count + local_ids, -1)
    local_orders = jnp.sum(slot_ints * order[:, None], axis=0)
    labels = lax.all_to_all(
        jnp.stack([element_ids, local_orders]), "dom", split_axis=1, concat_axis=1, tiled=True
    )
    moved_state, moved_adjoint = (
        lax.all_to_all(
            select_columns(coarse_state, slot_table), "dom", split_axis=2, concat_axis=2, tiled=True
        ),
        lax.all_to_all(
            select_columns(embedded + new_modes, slot_table),
            "dom",
            split_axis=2,
            concat_axis=2,
            tiled=True,
        ),
    )
    return (indicator, moved_state, moved_adjoint, labels[0], labels[1])


def solution(mesh):
    in_specs = (
        P(None, None, "dom"),
        P(None, None, "dom"),
        P("dom"),
        P(None, "dom"),
        P("dom", None),
        P(None, None, "dom"),
        P(),
        P(),
    )
    out_specs = (P("dom"), P(None, None, "dom"), P(None, None, "dom"), P("dom"), P("dom"))
    return jax.shard_map(body, mesh=mesh, in_specs=in_specs, out_specs=out_specs, check_vma=False)
```

profile of v0, /device:TPU:2, one launch (start us, length us, event | category | flops | bytes accessed | tf_op | source)
XLA Modules:
  0.0 148.6 jit_solution(2199932235944007820)
XLA Ops:
  1.6 1.4 broadcast_multiply_fusion
  4.0 1.9 %collective-permute-start = (f32[5,125,128]{2,1,0:T(8,128)}, f32[5,125,128]{2,1,0:T(8,128)}, u32[]{:S(2)}, u32[]{:S(2)}) collective-permute-start(f32[5,125,128]{2,1,0:T(8,128)} %get-tuple-element.41), channel_id=1, source_target_pairs={{0,1},{1,2},{2,3},{3,4},{4,5},{5,6},{6,7},{7,8},{8,9},{9,10},{10,1... | collective-permute-start | bytes 960008 | tf_op jit(solution)/shard_map/ppermute | solution.py:18
  5.9 7.9 %collective-permute-start.1 = (f32[5,125,128]{2,1,0:T(8,128)}, f32[5,125,128]{2,1,0:T(8,128)}, u32[]{:S(2)}, u32[]{:S(2)}) collective-permute-start(f32[5,125,128]{2,1,0:T(8,128)} %get-tuple-element.42), channel_id=1, source_target_pairs={{1,0},{2,1},{3,2},{4,3},{5,4},{6,5},{7,6},{8,7},{9,8},{10,9},{11,1... | collective-permute-start | bytes 960008 | tf_op jit(solution)/shard_map/ppermute | solution.py:21
  14.1 2.4 %select_reduce_fusion.2 = s32[2,128]{0,1:T(8,128)S(1)} fusion(s32[128,2,128]{0,1,2:T(2,128)S(1)} %fusion.95, s32[128,2]{0,1:T(2,128)S(1)} %slice.209, s32[2,128]{0,1:T(8,128)S(1)} %copy.52), kind=kLoop, calls=%fused_computation.131 | loop fusion | flops 163584 | bytes 134144 | tf_op jit(solution)/shard_map/reduce_sum | solution.py:129
  17.8 6.3 %all-to-all-start.2 = ((s32[2,128,4]{2,0,1:T(2,128)}), s32[2,128,4]{2,0,1:T(2,128)S(1)}, u32[]{:S(2)}, u32[]{:S(2)}) async-start(s32[2,128,4]{2,0,1:T(2,128)} %copy.56), calls=%async_computation.2 | async-start | bytes 262144 | tf_op jit(solution)/shard_map/all_to_all | solution.py:139
  27.8 1.9 %fusion.40 = f32[5,125,512]{2,1,0:T(8,128)} fusion(f32[5,125,256]{2,1,0:T(8,128)S(1)} %get-tuple-element.43, s32[256]{0:T(256)S(1)} %bitcast.172), kind=kOutput, calls=%fused_computation.57 | convolution fusion | flops 983171072 | bytes 1921024 | tf_op jit(solution)/shard_map/dot_general | solution.py:94
  30.4 1.1 reshape.1221
  31.5 1.4 pad.4
  32.9 1.1 reshape.1222
  38.8 1.1 fusion.5
  40.0 1.1 fusion.3
  41.3 1.2 fusion.18
  42.5 2.9 %copy.54 = f32[5,125,512]{1,0,2:T(8,128)} copy(f32[5,125,512]{2,1,0:T(8,128)} %fusion.40) | data formatting | bytes 2560000 | tf_op jit(solution)/shard_map/dot_general | solution.py:94
  45.4 10.2 %all-to-all-start = ((f32[5,125,512]{1,0,2:T(8,128)}), f32[5,125,512]{1,0,2:T(8,128)}, u32[]{:S(2)}, u32[]{:S(2)}) async-start(f32[5,125,512]{1,0,2:T(8,128)} %copy.54), calls=%async_computation | async-start | bytes 4194304 | tf_op jit(solution)/shard_map/all_to_all | solution.py:143
  56.8 3.5 %copy.55 = f32[5,216,512]{1,0,2:T(8,128)} copy(f32[5,216,512]{2,1,0:T(8,128)S(1)} %fusion.18) | data formatting | bytes 4423680 | tf_op jit(solution)/shard_map/dot_general | solution.py:94
  63.3 2.9 %convolution_bitcast_fusion = f32[6,5,25,512]{3,2,0,1:T(8,128)S(1)} fusion(f32[5,125,128]{2,1,0:T(8,128)} %collective-permute-done.1, f32[5,125,256]{2,1,0:T(8,128)S(1)} %get-tuple-element.43, f32[5,125,128]{2,1,0:T(8,128)} %collective-permute-done, f32[6,25,125]{2,1,0:T(8,128)} %copy-done.5), kind=kOutput, calls=%fused_computation | convolution fusion | flops 576640000 | bytes 2891000 | tf_op jit(solution)/shard_map/fqm,cme->fcqe/dot_general | solution.py:109
  67.4 18.1 %all-to-all-done = f32[5,125,512]{1,0,2:T(8,128)} async-done(((f32[5,125,512]{1,0,2:T(8,128)}), f32[5,125,512]{1,0,2:T(8,128)}, u32[]{:S(2)}, u32[]{:S(2)}) %all-to-all-start) | async-done | bytes 1280032 | tf_op jit(solution)/shard_map/all_to_all | solution.py:143
  85.5 6.0 %all-to-all-start.1 = ((f32[5,216,512]{1,0,2:T(8,128)}), f32[5,216,512]{1,0,2:T(8,128)}, u32[]{:S(2)}, u32[]{:S(2)}) async-start(f32[5,216,512]{1,0,2:T(8,128)} %copy.55), calls=%async_computation.1 | async-start | bytes 8388608 | tf_op jit(solution)/shard_map/all_to_all | solution.py:146
  96.8 1.4 slice_subtract_fusion
  99.2 1.5 convolution_bitcast_fusion.1
  100.7 1.4 fusion.11
  102.7 2.6 %copy.57 = f32[5,125,512]{2,1,0:T(8,128)} copy(f32[5,125,512]{1,0,2:T(8,128)} %all-to-all-done) | data formatting | bytes 2560000
  105.3 38.7 %all-to-all-done.1 = f32[5,216,512]{1,0,2:T(8,128)} async-done(((f32[5,216,512]{1,0,2:T(8,128)}), f32[5,216,512]{1,0,2:T(8,128)}, u32[]{:S(2)}, u32[]{:S(2)}) %all-to-all-start.1) | async-done | bytes 2211872 | tf_op jit(solution)/shard_map/all_to_all | solution.py:146
  144.0 4.6 %copy.58 = f32[5,216,512]{2,1,0:T(8,128)} copy(f32[5,216,512]{1,0,2:T(8,128)} %all-to-all-done.1) | data formatting | bytes 4423680
  (137 shorter events, 24.8 us)
Async XLA Ops:
  0.6 100.0 %copy-start = (f32[216,125]{1,0:T(8,128)S(1)}, f32[216,125]{1,0:T(8,128)}, u32[]{:S(2)}) copy-start(f32[216,125]{1,0:T(8,128)} %param.15) | copy-start | bytes 324004
  3.0 10.7 %copy-start.12 = (s32[256,1]{0,1:T(1,128)S(1)}, s32[256,1]{0,1:T(1,128)}, u32[]{:S(2)}) copy-start(s32[256,1]{0,1:T(1,128)} %param.12) | copy-start | bytes 3076
  3.1 13.6 %copy-start.18 = (s32[256]{0:T(256)S(1)}, s32[256]{0:T(256)}, u32[]{:S(2)}) copy-start(s32[256]{0:T(256)} %param.10) | copy-start | bytes 3076
  4.0 59.4 %collective-permute-start = (f32[5,125,128]{2,1,0:T(8,128)}, f32[5,125,128]{2,1,0:T(8,128)}, u32[]{:S(2)}, u32[]{:S(2)}) collective-permute-start(f32[5,125,128]{2,1,0:T(8,128)} %get-tuple-element.41), channel_id=1, source_target_pairs={{0,1},{1,2},{2,3},{3,4},{4,5},{5,6},{6,7},{7,8},{8,9},{9,10},{10,1... | collective-permute-start | bytes 960008 | tf_op jit(solution)/shard_map/ppermute | solution.py:18
  5.9 57.4 %collective-permute-start.1 = (f32[5,125,128]{2,1,0:T(8,128)}, f32[5,125,128]{2,1,0:T(8,128)}, u32[]{:S(2)}, u32[]{:S(2)}) collective-permute-start(f32[5,125,128]{2,1,0:T(8,128)} %get-tuple-element.42), channel_id=1, source_target_pairs={{1,0},{2,1},{3,2},{4,3},{5,4},{6,5},{7,6},{8,7},{9,8},{10,9},{11,1... | collective-permute-start | bytes 960008 | tf_op jit(solution)/shard_map/ppermute | solution.py:21
  17.1 12.7 %copy-start.9 = (f32[5,5,256]{2,1,0:T(8,128)S(1)}, f32[5,5,256]{2,1,0:T(8,128)}, u32[]{:S(2)}) copy-start(f32[5,5,256]{2,1,0:T(8,128)} %param.13) | copy-start | bytes 76804
  17.8 27.5 %all-to-all-start.2 = ((s32[2,128,4]{2,0,1:T(2,128)}), s32[2,128,4]{2,0,1:T(2,128)S(1)}, u32[]{:S(2)}, u32[]{:S(2)}) async-start(s32[2,128,4]{2,0,1:T(2,128)} %copy.56), calls=%async_computation.2 | async-start | bytes 262144 | tf_op jit(solution)/shard_map/all_to_all | solution.py:139
  32.9 4.8 %copy-start.4 = (f32[3,216,125]{2,1,0:T(8,128)S(1)}, f32[3,216,125]{2,1,0:T(8,128)}, u32[]{:S(2)}) copy-start(f32[3,216,125]{2,1,0:T(8,128)} %param.14) | copy-start | bytes 972004
  34.0 4.7 %copy-start.17 = (f32[1,216]{1,0:T(1,128)S(1)}, f32[1,216]{1,0:T(1,128)}, u32[]{:S(2)}) copy-start(f32[1,216]{1,0:T(1,128)} %get-tuple-element.57) | copy-start | bytes 2596
  36.8 3.1 %copy-start.10 = (f32[6,216,25]{1,2,0:T(8,128)}, f32[6,216,25]{1,2,0:T(8,128)S(1)}, u32[]{:S(2)}) copy-start(f32[6,216,25]{1,2,0:T(8,128)S(1)} %constant_dynamic-update-slice_fusion.6) | copy-start | bytes 388804
  45.4 10.3 %copy-start.7 = (s32[6,256]{1,0:T(8,128)S(1)}, s32[6,256]{1,0:T(8,128)}, u32[]{:S(2)}) copy-start(s32[6,256]{1,0:T(8,128)} %param.11) | copy-start | bytes 18436
  45.4 40.1 %all-to-all-start = ((f32[5,125,512]{1,0,2:T(8,128)}), f32[5,125,512]{1,0,2:T(8,128)}, u32[]{:S(2)}, u32[]{:S(2)}) async-start(f32[5,125,512]{1,0,2:T(8,128)} %copy.54), calls=%async_computation | async-start | bytes 4194304 | tf_op jit(solution)/shard_map/all_to_all | solution.py:143
  63.3 3.0 %copy-start.25 = (s32[1,256]{1,0:T(1,128)S(1)}, s32[1,256]{1,0:T(1,128)}, u32[]{:S(2)}) copy-start(s32[1,256]{1,0:T(1,128)} %get-tuple-element.55) | copy-start | bytes 3076
  63.3 3.0 %copy-start.27 = (pred[256]{0:T(512)(128)(4,1)S(1)}, pred[256]{0:T(512)(128)(4,1)}, u32[]{:S(2)}) copy-start(pred[256]{0:T(512)(128)(4,1)} %get-tuple-element.26) | copy-start | bytes 772
  67.3 24.2 %copy-start.16 = (s32[1,256]{1,0:T(1,128)S(1)}, s32[1,256]{1,0:T(1,128)}, u32[]{:S(2)}) copy-start(s32[1,256]{1,0:T(1,128)} %get-tuple-element.54) | copy-start | bytes 3076
  67.3 24.2 %copy-start.23 = (pred[256]{0:T(512)(128)(4,1)S(1)}, pred[256]{0:T(512)(128)(4,1)}, u32[]{:S(2)}) copy-start(pred[256]{0:T(512)(128)(4,1)} %get-tuple-element.25) | copy-start | bytes 772
  67.3 25.3 %copy-start.15 = (s32[1,256]{1,0:T(1,128)S(1)}, s32[1,256]{1,0:T(1,128)}, u32[]{:S(2)}) copy-start(s32[1,256]{1,0:T(1,128)} %get-tuple-element.53) | copy-start | bytes 3076
  67.3 25.3 %copy-start.22 = (pred[256]{0:T(512)(128)(4,1)S(1)}, pred[256]{0:T(512)(128)(4,1)}, u32[]{:S(2)}) copy-start(pred[256]{0:T(512)(128)(4,1)} %get-tuple-element.24) | copy-start | bytes 772
  67.4 26.3 %copy-start.14 = (s32[1,256]{1,0:T(1,128)S(1)}, s32[1,256]{1,0:T(1,128)}, u32[]{:S(2)}) copy-start(s32[1,256]{1,0:T(1,128)} %get-tuple-element.52) | copy-start | bytes 3076
  67.4 26.3 %copy-start.21 = (pred[256]{0:T(512)(128)(4,1)S(1)}, pred[256]{0:T(512)(128)(4,1)}, u32[]{:S(2)}) copy-start(pred[256]{0:T(512)(128)(4,1)} %get-tuple-element.23) | copy-start | bytes 772
  85.5 58.5 %all-to-all-start.1 = ((f32[5,216,512]{1,0,2:T(8,128)}), f32[5,216,512]{1,0,2:T(8,128)}, u32[]{:S(2)}, u32[]{:S(2)}) async-start(f32[5,216,512]{1,0,2:T(8,128)} %copy.55), calls=%async_computation.1 | async-start | bytes 8388608 | tf_op jit(solution)/shard_map/all_to_all | solution.py:146
  91.5 3.2 %copy-start.13 = (s32[1,256]{1,0:T(1,128)S(1)}, s32[1,256]{1,0:T(1,128)}, u32[]{:S(2)}) copy-start(s32[1,256]{1,0:T(1,128)} %get-tuple-element.51) | copy-start | bytes 3076
  91.5 3.2 %copy-start.20 = (pred[256]{0:T(512)(128)(4,1)S(1)}, pred[256]{0:T(512)(128)(4,1)}, u32[]{:S(2)}) copy-start(pred[256]{0:T(512)(128)(4,1)} %get-tuple-element.27) | copy-start | bytes 772
  91.5 4.2 %copy-start.19 = (pred[256]{0:T(512)(128)(4,1)S(1)}, pred[256]{0:T(512)(128)(4,1)}, u32[]{:S(2)}) copy-start(pred[256]{0:T(512)(128)(4,1)} %get-tuple-element.22) | copy-start | bytes 772
  (9 other events, 12.4 us)
where the time goes:
time: 151 us; the launch traced here: 149 us
  waiting for transfers between devices  56.8 us (38%)
  starting transfers between devices  32.3 us (21%)
  local copies, waits for them, and re-layouts  23.9 us (16%)
  matrix products  18.4 us (12%)
  other arithmetic  15.9 us (11%)
    all_to_all x1, waiting for transfers between devices, body(): lax.all_to_all(select_columns(embedded + new_modes, slot_table), 'dom', s...  38.7 us
    all_to_all x1, waiting for transfers between devices, body(): lax.all_to_all(select_columns(coarse_state, slot_table), 'dom', split_axi...  18.1 us
    all_to_all x1, starting transfers between devices, body(): lax.all_to_all(select_columns(coarse_state, slot_table), 'dom', split_axi...  10.2 us
    dot_general x8, matrix products, select_columns(): jnp.dot(flat, selector, precision=precise, preferred_element_type=jnp.flo...  9.3 us
    unnamed x59, local copies, waits for them, and re-layouts  8.97 us
    ppermute x1, starting transfers between devices, extended_2(): lax.ppermute(lax.slice_in_dim(block, 0, width, axis=dim), axis, backward)  7.86 us
    all_to_all x1, starting transfers between devices, body(): lax.all_to_all(jnp.stack([element_ids, local_orders]), 'dom', split_axis=...  6.31 us
    dot_general x2, local copies, waits for them, and re-layouts, select_columns(): jnp.dot(flat, selector, precision=precise, preferred_element_type=jnp.flo...  6.3 us
  transfers between devices with their start and end apart: 5, of which 2 were waited for; matrix products, arithmetic and copies ran while one was open for 33% of the time, Pallas kernels for 0%

commit v1 on v0

v1 whole, which is shorter than its diff:
```python
import functools
import jax
import jax.numpy as jnp
import numpy as np
from jax import lax
from jax.experimental import pallas as pl
from jax.experimental.pallas import tpu as pltpu
from jax.sharding import PartitionSpec as P

FIELDS = 5
MODES = 125
RICH = 216
KE = 256
CAP = 4
ND = 128
HALF = 128
QP = 32
VMEM = 48 * 1024 * 1024


def tables():
    m = np.arange(MODES)
    small = np.stack([m // 25, m // 5 % 5, m % 5])
    n = np.arange(RICH)
    rich = np.stack([n // 36, n // 6 % 6, n % 6])
    trace = np.zeros((6 * QP, MODES), np.float32)
    lift = np.zeros((RICH, 6 * QP), np.float32)
    for f in range(6):
        d = f // 2
        t1, t2 = [a for a in range(3) if a != d]
        s = -1.0 if f % 2 == 0 else 1.0
        trace[f * QP + small[t1] * 5 + small[t2], m] = s ** small[d]
        ok = (rich[t1] < 5) & (rich[t2] < 5)
        weight = s ** rich[d] * (2 * rich[d] + 1) * 0.5
        lift[n[ok], (f * QP + rich[t1] * 5 + rich[t2])[ok]] = weight[ok]
    embed = np.zeros((RICH, 128), np.float32)
    embed[small[0] * 36 + small[1] * 6 + small[2], m] = 1.0
    rich_top = rich.max(axis=0).astype(np.float32)[:, None]
    return trace, lift, embed, rich_top


TRACE, LIFT, EMBED, RICH_TOP = tables()


def dot(a, b):
    return lax.dot_general(a, b, (((1,), (0,)), ((), ())), preferred_element_type=jnp.float32)


def dot_nt(a, b):
    return lax.dot_general(a, b, (((1,), (1,)), ((), ())), preferred_element_type=jnp.float32)


def parts(x):
    high = x.astype(jnp.bfloat16)
    return high, (x - high.astype(jnp.float32)).astype(jnp.bfloat16)


def exact_dot(a, x):
    high, low = parts(x)
    return dot(a, high) + dot(a, low)


def dot_exact(x, a):
    high, low = parts(x)
    return dot(high, a) + dot(low, a)


def dot_three(a, x):
    a_high, a_low = a
    high, low = parts(x)
    return dot(a_high, high) + (dot(a_high, low) + dot(a_low, high))


def kept(order_row):
    m = lax.broadcasted_iota(jnp.int32, (MODES, KE), 0)
    i = (m * 41) >> 10
    rest = m - i * 25
    j = (rest * 13) >> 6
    k = rest - j * 5
    return jnp.maximum(jnp.maximum(i, j), k) <= order_row


def pack_kernel(order_ref, owner_ref, state_ref, adjoint_ref, out_ref, sel_ref, x_ref):
    @pl.when(pl.program_id(0) == 0)
    def _():
        hits = owner_ref[...] == lax.broadcasted_iota(jnp.int32, (ND, KE), 0)
        before = lax.broadcasted_iota(jnp.int32, (KE, KE), 0) < lax.broadcasted_iota(
            jnp.int32, (KE, KE), 1
        )
        ones = hits.astype(jnp.float32).astype(jnp.bfloat16)
        count = dot(ones, before.astype(jnp.float32).astype(jnp.bfloat16))
        for r in range(CAP):
            sel = jnp.where(hits & (count == float(r)), 1.0, 0.0)
            sel_ref[r * ND : (r + 1) * ND, :] = sel.astype(jnp.bfloat16)
        local = lax.broadcasted_iota(jnp.int32, (1, KE), 1)
        x_ref[125:126, :] = (local + 1).astype(jnp.float32)
        x_ref[126:127, :] = order_ref[...].astype(jnp.float32)
        x_ref[127:128, :] = jnp.zeros((1, KE), jnp.float32)
        x_ref[253:256, :] = jnp.zeros((3, KE), jnp.float32)

    keep = kept(order_ref[...])
    x_ref[0:MODES, :] = jnp.where(keep, state_ref[0], 0.0)
    x_ref[128 : 128 + MODES, :] = jnp.where(keep, adjoint_ref[0], 0.0)
    high, low = parts(x_ref[...])
    for r in range(CAP):
        sel = sel_ref[r * ND : (r + 1) * ND, :]
        rows = dot_nt(sel, high) + dot_nt(sel, low)
        out_ref[:, r, :] = rows[:, 0:128]
        out_ref[:, CAP + r, :] = rows[:, 128:256]


def pack(order_row, owner_row, state, adjoint):
    row = pl.BlockSpec((1, KE), lambda t: (0, 0))
    field = pl.BlockSpec((1, MODES, KE), lambda t: (t, 0, 0))
    return pl.pallas_call(
        pack_kernel,
        grid=(FIELDS,),
        in_specs=[row, row, field, field],
        out_specs=pl.BlockSpec((ND, 8, 128), lambda t: (0, t, 0)),
        out_shape=jax.ShapeDtypeStruct((ND, 8 * FIELDS, 128), jnp.float32),
        scratch_shapes=[
            pltpu.VMEM((CAP * ND, KE), jnp.bfloat16),
            pltpu.VMEM((256, KE), jnp.float32),
        ],
        compiler_params=pltpu.CompilerParams(vmem_limit_bytes=VMEM),
        name="pack",
    )(order_row, owner_row, state, adjoint)


def edge_kernel(order_ref, state_ref, trace_ref, first_ref, last_ref):
    keep = kept(order_ref[...])
    for c in range(FIELDS):
        coarse = jnp.where(keep, state_ref[c], 0.0)
        rows = exact_dot(trace_ref[0 : 2 * QP, :], coarse)
        for f in range(2):
            first_ref[f, c * QP : (c + 1) * QP, :] = rows[f * QP : (f + 1) * QP, :HALF]
            last_ref[f, c * QP : (c + 1) * QP, :] = rows[f * QP : (f + 1) * QP, KE - HALF :]


def edges(order_row, state, trace):
    shape = jax.ShapeDtypeStruct((2, FIELDS * QP, HALF), jnp.float32)
    return pl.pallas_call(
        edge_kernel,
        out_shape=(shape, shape),
        compiler_params=pltpu.CompilerParams(vmem_limit_bytes=VMEM),
        name="edges",
    )(order_row, state, trace)


def indicator_kernel(
    device_ref,
    order_ref,
    near_ref,
    state_ref,
    adjoint_ref,
    jacobian_ref,
    enrich_ref,
    volume_ref,
    before_ref,
    after_ref,
    trace_ref,
    lift_ref,
    top_ref,
    out_ref,
    rows_ref,
    traces_ref,
    jump_ref,
    flux_ref,
    coarse_ref,
):
    order_row = order_ref[...]
    keep = kept(order_row)
    start = device_ref[0] * KE
    for c in range(FIELDS):
        coarse = jnp.where(keep, state_ref[c], 0.0)
        coarse_ref[c] = coarse
        rows = exact_dot(trace_ref[...], coarse)
        for f in range(6):
            traces_ref[f, c * QP : (c + 1) * QP, :] = rows[f * QP : (f + 1) * QP, :]
    for f in range(6):
        near = near_ref[f : f + 1, :]
        local = jnp.where(near >= 0, near - start, -(1 << 20))

        def picks(count, shift):
            at = lax.broadcasted_iota(jnp.int32, (count, KE), 0)
            return jnp.where(at == local + shift, 1.0, 0.0).astype(jnp.bfloat16)

        other = f ^ 1
        found = dot_exact(traces_ref[other], picks(KE, 0))
        if f < 2:
            found = found + dot_exact(before_ref[other], picks(HALF, HALF))
            found = found + dot_exact(after_ref[other], picks(HALF, -KE))
        jump_ref[f] = found - traces_ref[f]
    top = top_ref[...]
    enrich = jnp.where(
        top == 3.0,
        enrich_ref[0],
        jnp.where(top == 4.0, enrich_ref[1], jnp.where(top == 5.0, enrich_ref[2], 0.0)),
    )
    enrich_parts = parts(enrich)
    rows_ref[0:RICH, 0:MODES] = enrich_parts[0]
    rows_ref[RICH:, 0:MODES] = enrich_parts[1]
    rows_ref[:, MODES:] = jnp.zeros((2 * RICH, 3), jnp.bfloat16)
    volume_parts = parts(volume_ref[...])
    new_mask = top == order_row.astype(jnp.float32) + 1.0
    total = jnp.zeros((RICH, KE), jnp.float32)
    for c in range(FIELDS):
        factors = jacobian_ref[c]
        weighted = factors[0:1, :] * coarse_ref[0]
        for h in range(1, FIELDS):
            weighted = weighted + factors[h : h + 1, :] * coarse_ref[h]
        for f in range(6):
            flux = factors[0:1, :] * jump_ref[f, 0:QP, :]
            for h in range(1, FIELDS):
                flux = flux + factors[h : h + 1, :] * jump_ref[f, h * QP : (h + 1) * QP, :]
            flux_ref[f * QP : (f + 1) * QP, :] = flux
        residual = dot_three(volume_parts, weighted) + exact_dot(lift_ref[...], flux_ref[...])
        new = dot_three(enrich_parts, jnp.where(keep, adjoint_ref[c], 0.0))
        total = total + jnp.where(new_mask, new, 0.0) * residual
    out_ref[...] = jnp.abs(jnp.sum(total, axis=0, keepdims=True)) * (1.0 / 216.0)


def indicators(device, order_row, near, state, adjoint, jacobian, enrich, volume, before, after):
    space = pl.BlockSpec(memory_space=pltpu.VMEM)
    return pl.pallas_call(
        indicator_kernel,
        in_specs=[pl.BlockSpec(memory_space=pltpu.SMEM)] + [space] * 12,
        out_specs=(space, space),
        out_shape=(
            jax.ShapeDtypeStruct((1, KE), jnp.float32),
            jax.ShapeDtypeStruct((2 * RICH, 128), jnp.bfloat16),
        ),
        scratch_shapes=[
            pltpu.VMEM((6, FIELDS * QP, KE), jnp.float32),
            pltpu.VMEM((6, FIELDS * QP, KE), jnp.float32),
            pltpu.VMEM((6 * QP, KE), jnp.float32),
            pltpu.VMEM((FIELDS, MODES, KE), jnp.float32),
        ],
        compiler_params=pltpu.CompilerParams(vmem_limit_bytes=VMEM),
        name="indicators",
    )(
        device,
        order_row,
        near,
        state,
        adjoint,
        jacobian,
        enrich,
        volume,
        before,
        after,
        jnp.asarray(TRACE, jnp.bfloat16),
        jnp.asarray(LIFT, jnp.bfloat16),
        jnp.asarray(RICH_TOP),
    )


def unpack_kernel(in_ref, enrich_ref, embed_ref, eye_ref, top_ref, state_ref, adjoint_ref, ids_ref, orders_ref):
    block = in_ref[...].reshape(ND // 2, 2, 8, 128)
    even, odd = block[:, 0], block[:, 1]
    upper = lax.broadcasted_iota(jnp.int32, even.shape, 1) >= CAP
    slots = ND * CAP
    state = jnp.where(upper, pltpu.roll(odd, CAP, 1), even).reshape(slots, 128)
    adjoint = jnp.where(upper, odd, pltpu.roll(even, CAP, 1)).reshape(slots, 128)
    high, low = parts(state)
    eye = eye_ref[...]
    moved = dot_nt(eye, high) + dot_nt(eye, low)
    state_ref[0] = moved[0:MODES, :]
    order_row = moved[126:127, :]
    high, low = parts(adjoint)
    embed = embed_ref[...]
    old = dot_nt(embed, high) + dot_nt(embed, low)
    top_rows, bottom = enrich_ref[0:RICH, :], enrich_ref[RICH:, :]
    new = dot_nt(top_rows, high) + (dot_nt(top_rows, low) + dot_nt(bottom, high))
    adjoint_ref[0] = old + jnp.where(top_ref[...] == order_row + 1.0, new, 0.0)

    @pl.when(pl.program_id(0) == 0)
    def _():
        id_row = moved[125:126, :].astype(jnp.int32)
        first = (lax.broadcasted_iota(jnp.int32, (1, slots), 1) >> 2) * KE
        ids_ref[...] = jnp.where(id_row > 0, first + id_row - 1, -1)
        orders_ref[...] = order_row.astype(jnp.int32)


def unpack(received, enrich_rows):
    slots = ND * CAP
    whole = lambda a: pl.BlockSpec(a, lambda t: (0,) * len(a))
    return pl.pallas_call(
        unpack_kernel,
        grid=(FIELDS,),
        in_specs=[
            pl.BlockSpec((ND, 8, 128), lambda t: (0, t, 0)),
            whole((2 * RICH, 128)),
            whole((RICH, 128)),
            whole((128, 128)),
            whole((RICH, 1)),
        ],
        out_specs=(
            pl.BlockSpec((1, MODES, slots), lambda t: (t, 0, 0)),
            pl.BlockSpec((1, RICH, slots), lambda t: (t, 0, 0)),
            whole((1, slots)),
            whole((1, slots)),
        ),
        out_shape=(
            jax.ShapeDtypeStruct((FIELDS, MODES, slots), jnp.float32),
            jax.ShapeDtypeStruct((FIELDS, RICH, slots), jnp.float32),
            jax.ShapeDtypeStruct((1, slots), jnp.int32),
            jax.ShapeDtypeStruct((1, slots), jnp.int32),
        ),
        compiler_params=pltpu.CompilerParams(vmem_limit_bytes=VMEM),
        name="unpack",
    )(
        received,
        enrich_rows,
        jnp.asarray(EMBED, jnp.bfloat16),
        jnp.asarray(np.eye(128), jnp.bfloat16),
        jnp.asarray(RICH_TOP),
    )


def body(state, adjoint, order, neighbours, owner, jacobian, enrich, volume):
    device = lax.axis_index("dom")
    order_row = order.reshape(1, KE)
    message = pack(order_row, owner.reshape(1, KE), state, adjoint)
    received = lax.all_to_all(message, "dom", split_axis=0, concat_axis=0, tiled=True)
    first, last = edges(order_row, state, jnp.asarray(TRACE, jnp.bfloat16))
    up = [(i, i + 1) for i in range(ND - 1)]
    down = [(i + 1, i) for i in range(ND - 1)]
    before = lax.ppermute(last, "dom", up)
    after = lax.ppermute(first, "dom", down)
    indicator, enrich_rows = indicators(
        device.reshape(1),
        order_row,
        neighbours,
        state,
        adjoint,
        jacobian,
        enrich,
        volume,
        before,
        after,
    )
    moved_state, moved_adjoint, ids, orders = unpack(received, enrich_rows)
    return (
        indicator.reshape(KE),
        moved_state,
        moved_adjoint,
        ids.reshape(ND * CAP),
        orders.reshape(ND * CAP),
    )


def solution(mesh):
    wide = P(None, None, "dom")
    in_specs = (wide, wide, P("dom"), P(None, "dom"), P("dom", None), wide, P(), P())
    out_specs = (P("dom"), wide, wide, P("dom"), P("dom"))
    return jax.shard_map(body, mesh=mesh, in_specs=in_specs, out_specs=out_specs, check_vma=False)
```

time: 151 us -> 73.5 us (0.49); the launches traced: 149 us -> 72.8 us
  waiting for transfers between devices: 56.8 us -> 26.1 us
  matrix products: 18.4 us -> 0 us
  other arithmetic: 15.9 us -> 0 us
  Pallas kernels: 0 us -> 13.1 us
  starting transfers between devices: 32.3 us -> 20.3 us
  local copies, waits for them, and re-layouts: 23.9 us -> 12.6 us
    all_to_all x3 -> x1, waiting for transfers between devices: 56.8 us -> 0.01 us  [body(): lax.all_to_all(message, 'dom', split_axis=0, concat_axis=0, tiled=True)]
    ppermute x2, waiting for transfers between devices: 0.01 us -> 26.1 us  [the longest x1 26.1 us: body(): before = lax.ppermute(last, 'dom', up)]
    dot_general x14 -> x0, matrix products: 18.4 us -> none  [the longest x8 9.3 us: select_columns(): jnp.dot(flat, selector, precision=precise, preferred_element_type=jnp.flo...]
    pallas_call x0 -> x4, Pallas kernels: none -> 13.1 us  [the longest x1 4.38 us: unpack(): pl.pallas_call(unpack_kernel, grid=(FIELDS,), in_specs=[pl.BlockSpec((ND,...]
    all_to_all x3 -> x1, starting transfers between devices: 22.6 us -> 10.5 us  [body(): lax.all_to_all(message, 'dom', split_axis=0, concat_axis=0, tiled=True)]
    dot_general x2 -> x0, local copies, waits for them, and re-layouts: 6.3 us -> none  [select_columns(): jnp.dot(flat, selector, precision=precise, preferred_element_type=jnp.flo...]
    mul x11 -> x0, other arithmetic: 5.35 us -> none  [the longest x6 2.35 us: mode_tables(): lift_weight = rich_parity * (2 * rich_normal + 1).astype(jnp.float32) * 0.5]
    unnamed x59 -> x38, local copies, waits for them, and re-layouts: 8.97 us -> 12.6 us
  transfers between devices with their start and end apart: 5 -> 3, of which waited for: 2 -> 1; matrix products, arithmetic and copies ran while one was open for 33% -> 0% of each run, Pallas kernels for 0% -> 7%
where the time goes in v1:
time: 73.5 us; the launch traced here: 72.8 us
  waiting for transfers between devices  26.1 us (36%)
  starting transfers between devices  20.3 us (28%)
  Pallas kernels  13.1 us (18%)
  local copies, waits for them, and re-layouts  12.6 us (17%)
  between operations  0.75 us (1%)
    ppermute x1, waiting for transfers between devices, body(): before = lax.ppermute(last, 'dom', up)  26.1 us
    unnamed x38, local copies, waits for them, and re-layouts  12.6 us
    all_to_all x1, starting transfers between devices, body(): lax.all_to_all(message, 'dom', split_axis=0, concat_axis=0, tiled=True)  10.5 us
    ppermute x1, starting transfers between devices, body(): after = lax.ppermute(first, 'dom', down)  7.73 us
    pallas_call x1, Pallas kernels, unpack(): pl.pallas_call(unpack_kernel, grid=(FIELDS,), in_specs=[pl.BlockSpec((ND,...  4.38 us
    pallas_call x1, Pallas kernels, indicators(): pl.pallas_call(indicator_kernel, in_specs=[pl.BlockSpec(memory_space=pltp...  4.12 us
    pallas_call x1, Pallas kernels, pack(): pl.pallas_call(pack_kernel, grid=(FIELDS,), in_specs=[row, row, field, fi...  3.57 us
    ppermute x1, starting transfers between devices, body(): before = lax.ppermute(last, 'dom', up)  2.05 us
  transfers between devices with their start and end apart: 3, of which 1 were waited for; matrix products, arithmetic and copies ran while one was open for 0% of the time, Pallas kernels for 7%

profile of v1, /device:TPU:2, one launch (start us, length us, event | category | flops | bytes accessed | tf_op | source)
XLA Modules:
  0.0 72.8 jit_solution(8268457467316343259)
XLA Ops:
  0.6 0.0 copy-start.1
  0.6 1.1 %copy-done.1 = f32[5,125,256]{2,1,0:T(8,128)S(1)} copy-done((f32[5,125,256]{2,1,0:T(8,128)S(1)}, f32[5,125,256]{2,1,0:T(8,128)}, u32[]{:S(2)}) %copy-start.1) | copy-done | bytes 640024
  1.7 1.1 %copy-done.3 = f32[5,125,256]{2,1,0:T(8,128)S(1)} copy-done((f32[5,125,256]{2,1,0:T(8,128)S(1)}, f32[5,125,256]{2,1,0:T(8,128)}, u32[]{:S(2)}) %copy-start.3) | copy-done | bytes 640024
  2.8 0.7 copy-done.15
  3.5 0.7 copy-done.18
  4.2 3.6 %pack.1 = f32[128,40,128]{2,1,0:T(8,128)S(1)} custom-call(s32[1,256]{1,0:T(1,128)S(1)} %bitcast.6, s32[1,256]{1,0:T(1,128)S(1)} %bitcast.9, f32[5,125,256]{2,1,0:T(8,128)S(1)} %copy-done.1, f32[5,125,256]{2,1,0:T(8,128)S(1)} %copy-done.3), custom_call_target="tpu_custom_call" | custom-call | tf_op jit(solution)/shard_map/pack/pallas_call | solution.py:115
  7.8 1.5 %copy-done = f32[128,40,128]{2,1,0:T(8,128)} copy-done((f32[128,40,128]{2,1,0:T(8,128)}, f32[128,40,128]{2,1,0:T(8,128)S(1)}, u32[]{:S(2)}) %copy-start) | copy-done | bytes 2621464
  9.3 10.5 %all-to-all-start = ((f32[128,40,128]{2,1,0:T(8,128)}), f32[128,40,128]{2,1,0:T(8,128)S(1)}, u32[]{:S(2)}, u32[]{:S(2)}) async-start(f32[128,40,128]{2,1,0:T(8,128)} %copy-done), calls=%async_computation | async-start | bytes 5242880 | tf_op jit(solution)/shard_map/all_to_all | solution.py:325
  19.8 1.1 %edges.1 = (f32[2,160,128]{2,1,0:T(8,128)}, f32[2,160,128]{2,1,0:T(8,128)}) custom-call(s32[1,256]{1,0:T(1,128)S(1)} %bitcast.7, f32[5,125,256]{2,1,0:T(8,128)S(1)} %copy-done.2, bf16[192,125]{1,0:T(8,128)(2,1)S(1)} %copy-done.7), custom_call_target="tpu_custom_call" | custom-call | tf_op jit(solution)/shard_map/edges/pallas_call | solution.py:142
  20.9 2.0 %collective-permute-start = (f32[2,160,128]{2,1,0:T(8,128)}, f32[2,160,128]{2,1,0:T(8,128)}, u32[]{:S(2)}, u32[]{:S(2)}) collective-permute-start(f32[2,160,128]{2,1,0:T(8,128)} %get-tuple-element.13), channel_id=1, source_target_pairs={{0,1},{1,2},{2,3},{3,4},{4,5},{5,6},{6,7},{7,8},{8,9},{9,10},{10,1... | collective-permute-start | bytes 491528 | tf_op jit(solution)/shard_map/ppermute | solution.py:329
  23.0 7.7 %collective-permute-start.1 = (f32[2,160,128]{2,1,0:T(8,128)}, f32[2,160,128]{2,1,0:T(8,128)}, u32[]{:S(2)}, u32[]{:S(2)}) collective-permute-start(f32[2,160,128]{2,1,0:T(8,128)} %get-tuple-element.14), channel_id=1, source_target_pairs={{1,0},{2,1},{3,2},{4,3},{5,4},{6,5},{7,6},{8,7},{9,8},{10,9},{11,1... | collective-permute-start | bytes 491528 | tf_op jit(solution)/shard_map/ppermute | solution.py:330
  30.7 26.1 %collective-permute-done.before_ref = f32[2,160,128]{2,1,0:T(8,128)} collective-permute-done((f32[2,160,128]{2,1,0:T(8,128)}, f32[2,160,128]{2,1,0:T(8,128)}, u32[]{:S(2)}, u32[]{:S(2)}) %collective-permute-start) | collective-permute-done | bytes 163872 | tf_op jit(solution)/shard_map/ppermute | solution.py:329
  56.8 0.0 copy-start.4
  56.8 1.1 %copy-done.4 = f32[5,125,256]{2,1,0:T(8,128)S(1)} copy-done((f32[5,125,256]{2,1,0:T(8,128)S(1)}, f32[5,125,256]{2,1,0:T(8,128)}, u32[]{:S(2)}) %copy-start.4) | copy-done | bytes 640024
  57.9 1.0 %copy-done.6 = f32[3,216,125]{2,1,0:T(8,128)S(1)} copy-done((f32[3,216,125]{2,1,0:T(8,128)S(1)}, f32[3,216,125]{2,1,0:T(8,128)}, u32[]{:S(2)}) %copy-start.6) | copy-done | bytes 324024
  58.8 0.9 %copy-done.9 = bf16[216,192]{1,0:T(8,128)(2,1)S(1)} copy-done((bf16[216,192]{1,0:T(8,128)(2,1)S(1)}, bf16[216,192]{1,0:T(8,128)(2,1)}, u32[]{:S(2)}) %copy-start.9) | copy-done | bytes 82968
  59.7 0.8 %copy-done.13 = f32[5,5,256]{2,1,0:T(8,128)S(1)} copy-done((f32[5,5,256]{2,1,0:T(8,128)S(1)}, f32[5,5,256]{2,1,0:T(8,128)}, u32[]{:S(2)}) %copy-start.13) | copy-done | bytes 25624
  60.5 0.7 copy-done.17
  61.2 4.1 %indicators.1 = (f32[1,256]{1,0:T(1,128)}, bf16[432,128]{1,0:T(8,128)(2,1)S(1)}) custom-call(s32[1]{0:T(128)} %bitcast.device_ref, s32[1,256]{1,0:T(1,128)S(1)} %bitcast.8, s32[6,256]{1,0:T(8,128)S(1)} %copy-done.17, f32[5,125,256]{2,1,0:T(8,128)S(1)} %copy-done.2, f32[5,125,256]{2,1,0:T(8,128)S(1)} %copy-done.4, f32[5,5,256]{2,1,0:T(8,128)S(1)} %copy-done.13, ...), custom_call_target="tpu_custom_call" | custom-call | tf_op jit(solution)/shard_map/indicators/pallas_call | solution.py:225
  65.3 0.6 copy-done.10
  66.0 0.9 %copy-done.11 = bf16[432,128]{1,0:T(8,128)(2,1)S(1)} copy-done((bf16[432,128]{1,0:T(8,128)(2,1)S(1)}, bf16[432,128]{1,0:T(8,128)(2,1)}, u32[]{:S(2)}) %copy-start.11) | copy-done | bytes 110616
  66.9 0.8 %copy-done.12 = bf16[216,128]{1,0:T(8,128)(2,1)S(1)} copy-done((bf16[216,128]{1,0:T(8,128)(2,1)S(1)}, bf16[216,128]{1,0:T(8,128)(2,1)}, u32[]{:S(2)}) %copy-start.12) | copy-done | bytes 55320
  67.7 0.8 %copy-done.14 = bf16[128,128]{1,0:T(8,128)(2,1)S(1)} copy-done((bf16[128,128]{1,0:T(8,128)(2,1)S(1)}, bf16[128,128]{1,0:T(8,128)(2,1)}, u32[]{:S(2)}) %copy-start.14) | copy-done | bytes 32792
  68.4 4.4 %unpack.1 = (f32[5,125,512]{2,1,0:T(8,128)}, f32[5,216,512]{2,1,0:T(8,128)}, s32[1,512]{1,0:T(1,128)}, s32[1,512]{1,0:T(1,128)}) custom-call(f32[128,40,128]{2,1,0:T(8,128)S(1)} %all-to-all-done.in_ref, bf16[432,128]{1,0:T(8,128)(2,1)S(1)} %copy-done.11, bf16[216,128]{1,0:T(8,128)(2,1)S(1)} %copy-done.12, bf16[128,128]{1,0:T(8,128)(2,1)S(1)} %copy-done.14, ...), custom_call_target="tpu_custom_call" | custom-call | tf_op jit(solution)/shard_map/unpack/pallas_call | solution.py:288
  (24 shorter events, 0.0 us)
Async XLA Ops:
  0.6 1.1 %copy-start.1 = (f32[5,125,256]{2,1,0:T(8,128)S(1)}, f32[5,125,256]{2,1,0:T(8,128)}, u32[]{:S(2)}) copy-start(f32[5,125,256]{2,1,0:T(8,128)} %state_ref.5) | copy-start | bytes 1920004
  1.7 1.1 %copy-start.3 = (f32[5,125,256]{2,1,0:T(8,128)S(1)}, f32[5,125,256]{2,1,0:T(8,128)}, u32[]{:S(2)}) copy-start(f32[5,125,256]{2,1,0:T(8,128)} %adjoint_ref.3) | copy-start | bytes 1920004
  2.8 0.7 copy-start.15
  3.5 0.7 copy-start.18
  7.7 1.5 %copy-start = (f32[128,40,128]{2,1,0:T(8,128)}, f32[128,40,128]{2,1,0:T(8,128)S(1)}, u32[]{:S(2)}) copy-start(f32[128,40,128]{2,1,0:T(8,128)S(1)} %pack.1) | copy-start | bytes 7864324
  9.2 10.6 %copy-start.2 = (f32[5,125,256]{2,1,0:T(8,128)S(1)}, f32[5,125,256]{2,1,0:T(8,128)}, u32[]{:S(2)}) copy-start(f32[5,125,256]{2,1,0:T(8,128)} %state_ref.5) | copy-start | bytes 1920004
  9.2 10.6 %copy-start.7 = (bf16[192,125]{1,0:T(8,128)(2,1)S(1)}, bf16[192,125]{1,0:T(8,128)(2,1)}, u32[]{:S(2)}) copy-start(bf16[192,125]{1,0:T(8,128)(2,1)} %constant.14.clone.trace_ref) | copy-start | bytes 144004
  9.3 10.6 %copy-start.16 = (s32[256]{0:T(256)S(1)}, s32[256]{0:T(256)}, u32[]{:S(2)}) copy-start(s32[256]{0:T(256)} %param.16) | copy-start | bytes 3076
  9.3 47.5 %copy-start.5 = (f32[216,1]{1,0:T(8,128)S(1)}, f32[216,1]{1,0:T(8,128)}, u32[]{:S(2)}) copy-start(f32[216,1]{1,0:T(8,128)} %constant.16.clone.top_ref) | copy-start | bytes 2596
  9.3 47.5 %copy-start.8 = (f32[216,125]{1,0:T(8,128)S(1)}, f32[216,125]{1,0:T(8,128)}, u32[]{:S(2)}) copy-start(f32[216,125]{1,0:T(8,128)} %volume_ref.1) | copy-start | bytes 324004
  9.3 56.7 %all-to-all-start = ((f32[128,40,128]{2,1,0:T(8,128)}), f32[128,40,128]{2,1,0:T(8,128)S(1)}, u32[]{:S(2)}, u32[]{:S(2)}) async-start(f32[128,40,128]{2,1,0:T(8,128)} %copy-done), calls=%async_computation | async-start | bytes 5242880 | tf_op jit(solution)/shard_map/all_to_all | solution.py:325
  20.9 35.9 %collective-permute-start = (f32[2,160,128]{2,1,0:T(8,128)}, f32[2,160,128]{2,1,0:T(8,128)}, u32[]{:S(2)}, u32[]{:S(2)}) collective-permute-start(f32[2,160,128]{2,1,0:T(8,128)} %get-tuple-element.13), channel_id=1, source_target_pairs={{0,1},{1,2},{2,3},{3,4},{4,5},{5,6},{6,7},{7,8},{8,9},{9,10},{10,1... | collective-permute-start | bytes 491528 | tf_op jit(solution)/shard_map/ppermute | solution.py:329
  23.0 33.8 %collective-permute-start.1 = (f32[2,160,128]{2,1,0:T(8,128)}, f32[2,160,128]{2,1,0:T(8,128)}, u32[]{:S(2)}, u32[]{:S(2)}) collective-permute-start(f32[2,160,128]{2,1,0:T(8,128)} %get-tuple-element.14), channel_id=1, source_target_pairs={{1,0},{2,1},{3,2},{4,3},{5,4},{6,5},{7,6},{8,7},{9,8},{10,9},{11,1... | collective-permute-start | bytes 491528 | tf_op jit(solution)/shard_map/ppermute | solution.py:330
  56.8 1.1 %copy-start.4 = (f32[5,125,256]{2,1,0:T(8,128)S(1)}, f32[5,125,256]{2,1,0:T(8,128)}, u32[]{:S(2)}) copy-start(f32[5,125,256]{2,1,0:T(8,128)} %adjoint_ref.3) | copy-start | bytes 1920004
  57.9 1.0 %copy-start.6 = (f32[3,216,125]{2,1,0:T(8,128)S(1)}, f32[3,216,125]{2,1,0:T(8,128)}, u32[]{:S(2)}) copy-start(f32[3,216,125]{2,1,0:T(8,128)} %enrich_ref.1) | copy-start | bytes 972004
  58.8 0.9 %copy-start.9 = (bf16[216,192]{1,0:T(8,128)(2,1)S(1)}, bf16[216,192]{1,0:T(8,128)(2,1)}, u32[]{:S(2)}) copy-start(bf16[216,192]{1,0:T(8,128)(2,1)} %constant.15.clone.lift_ref) | copy-start | bytes 248836
  59.7 0.8 %copy-start.13 = (f32[5,5,256]{2,1,0:T(8,128)S(1)}, f32[5,5,256]{2,1,0:T(8,128)}, u32[]{:S(2)}) copy-start(f32[5,5,256]{2,1,0:T(8,128)} %jacobian_ref.1) | copy-start | bytes 76804
  60.5 0.7 copy-start.17
  65.3 0.6 copy-start.10
  66.0 0.9 %copy-start.11 = (bf16[432,128]{1,0:T(8,128)(2,1)S(1)}, bf16[432,128]{1,0:T(8,128)(2,1)}, u32[]{:S(2)}) copy-start(bf16[432,128]{1,0:T(8,128)(2,1)} %copy-done.10) | copy-start | bytes 331780
  66.9 0.8 %copy-start.12 = (bf16[216,128]{1,0:T(8,128)(2,1)S(1)}, bf16[216,128]{1,0:T(8,128)(2,1)}, u32[]{:S(2)}) copy-start(bf16[216,128]{1,0:T(8,128)(2,1)} %constant.17.clone.embed_ref) | copy-start | bytes 165892
  67.7 0.8 %copy-start.14 = (bf16[128,128]{1,0:T(8,128)(2,1)S(1)}, bf16[128,128]{1,0:T(8,128)(2,1)}, u32[]{:S(2)}) copy-start(bf16[128,128]{1,0:T(8,128)(2,1)} %constant.18.clone.eye_ref) | copy-start | bytes 98308

commit v2 on v1

v2 whole, which is shorter than its diff:
```python
import jax
import jax.numpy as jnp
import numpy as np
from jax import lax
from jax.experimental import pallas as pl
from jax.experimental.pallas import tpu as pltpu
from jax.sharding import PartitionSpec as P

FIELDS = 5
MODES = 125
RICH = 216
KE = 256
CAP = 4
ND = 128
HALF = 128
QP = 32
VMEM = 48 * 1024 * 1024


def tables():
    m = np.arange(MODES)
    small = np.stack([m // 25, m // 5 % 5, m % 5])
    n = np.arange(RICH)
    rich = np.stack([n // 36, n // 6 % 6, n % 6])
    trace = np.zeros((6 * QP, MODES), np.float32)
    lift = np.zeros((RICH, 6 * QP), np.float32)
    for f in range(6):
        d = f // 2
        t1, t2 = [a for a in range(3) if a != d]
        s = -1.0 if f % 2 == 0 else 1.0
        trace[f * QP + small[t1] * 5 + small[t2], m] = s ** small[d]
        ok = (rich[t1] < 5) & (rich[t2] < 5)
        weight = s ** rich[d] * (2 * rich[d] + 1) * 0.5
        lift[n[ok], (f * QP + rich[t1] * 5 + rich[t2])[ok]] = weight[ok]
    rich_top = rich.max(axis=0).astype(np.float32)[:, None]
    return trace, lift, rich_top


TRACE, LIFT, RICH_TOP = tables()


def hbm(x):
    return pltpu.with_memory_space_constraint(x, pltpu.HBM)


def dot(a, b):
    return lax.dot_general(a, b, (((1,), (0,)), ((), ())), preferred_element_type=jnp.float32)


def dot_nt(a, b):
    return lax.dot_general(a, b, (((1,), (1,)), ((), ())), preferred_element_type=jnp.float32)


def parts(x):
    high = x.astype(jnp.bfloat16)
    return high, (x - high.astype(jnp.float32)).astype(jnp.bfloat16)


def exact_dot(a, x):
    high, low = parts(x)
    return dot(a, high) + dot(a, low)


def dot_exact(x, a):
    high, low = parts(x)
    return dot(high, a) + dot(low, a)


def dot_three(a, x):
    a_high, a_low = a
    high, low = parts(x)
    return dot(a_high, high) + (dot(a_high, low) + dot(a_low, high))


def kept(order_row):
    m = lax.broadcasted_iota(jnp.int32, (MODES, KE), 0)
    i = (m * 41) >> 10
    rest = m - i * 25
    j = (rest * 13) >> 6
    k = rest - j * 5
    return jnp.maximum(jnp.maximum(i, j), k) <= order_row


def pack_kernel(
    order_hbm,
    owner_hbm,
    state_hbm,
    adjoint_hbm,
    out_hbm,
    order_ref,
    owner_ref,
    state_ref,
    adjoint_ref,
    x_ref,
    out_ref,
    in_sems,
    out_sems,
):
    small = [
        pltpu.make_async_copy(order_hbm, order_ref, in_sems.at[0]),
        pltpu.make_async_copy(owner_hbm, owner_ref, in_sems.at[1]),
    ]
    fields = [
        (
            pltpu.make_async_copy(state_hbm.at[t], state_ref.at[t], in_sems.at[2 + 2 * t]),
            pltpu.make_async_copy(adjoint_hbm.at[t], adjoint_ref.at[t], in_sems.at[3 + 2 * t]),
        )
        for t in range(FIELDS)
    ]
    for copy in small:
        copy.start()
    for pair in fields:
        for copy in pair:
            copy.start()
    before = lax.broadcasted_iota(jnp.int32, (KE, KE), 0) < lax.broadcasted_iota(
        jnp.int32, (KE, KE), 1
    )
    before = jnp.where(before, 1.0, 0.0).astype(jnp.bfloat16)
    local = lax.broadcasted_iota(jnp.int32, (1, KE), 1)
    x_ref[125:126, :] = (local + 1).astype(jnp.float32)
    x_ref[127:128, :] = jnp.zeros((1, KE), jnp.float32)
    x_ref[253:256, :] = jnp.zeros((3, KE), jnp.float32)
    for copy in small:
        copy.wait()
    order_row = order_ref[...]
    x_ref[126:127, :] = order_row.astype(jnp.float32)
    hits = owner_ref[...] == lax.broadcasted_iota(jnp.int32, (ND, KE), 0)
    count = dot(jnp.where(hits, 1.0, 0.0).astype(jnp.bfloat16), before)
    sel = jnp.concatenate(
        [
            jnp.where(hits & (count == float(r)), 1.0, 0.0).astype(jnp.bfloat16)
            for r in range(CAP)
        ],
        axis=0,
    )
    keep = kept(order_row)
    sends = []
    for t in range(FIELDS):
        for copy in fields[t]:
            copy.wait()
        x_ref[0:MODES, :] = jnp.where(keep, state_ref[t], 0.0)
        x_ref[128 : 128 + MODES, :] = jnp.where(keep, adjoint_ref[t], 0.0)
        high, low = parts(x_ref[...])
        rows = dot_nt(sel, high) + dot_nt(sel, low)
        for r in range(CAP):
            out_ref[t, :, r, :] = rows[r * ND : (r + 1) * ND, 0:128]
            out_ref[t, :, CAP + r, :] = rows[r * ND : (r + 1) * ND, 128:256]
        send = pltpu.make_async_copy(
            out_ref.at[t], out_hbm.at[:, pl.ds(8 * t, 8), :], out_sems.at[t]
        )
        send.start()
        sends.append(send)
    for send in sends:
        send.wait()


def pack(order_row, owner_row, state, adjoint):
    far = pl.BlockSpec(memory_space=pltpu.HBM)
    return pl.pallas_call(
        pack_kernel,
        in_specs=[far] * 4,
        out_specs=far,
        out_shape=pltpu.HBM((ND, 8 * FIELDS, 128), jnp.float32),
        scratch_shapes=[
            pltpu.VMEM((1, KE), jnp.int32),
            pltpu.VMEM((1, KE), jnp.int32),
            pltpu.VMEM((FIELDS, MODES, KE), jnp.float32),
            pltpu.VMEM((FIELDS, MODES, KE), jnp.float32),
            pltpu.VMEM((256, KE), jnp.float32),
            pltpu.VMEM((FIELDS, ND, 8, 128), jnp.float32),
            pltpu.SemaphoreType.DMA((2 + 2 * FIELDS,)),
            pltpu.SemaphoreType.DMA((FIELDS,)),
        ],
        compiler_params=pltpu.CompilerParams(vmem_limit_bytes=VMEM),
        name="pack",
    )(hbm(order_row), hbm(owner_row), hbm(state), hbm(adjoint))


def edge_kernel(order_ref, state_ref, trace_ref, first_ref, last_ref):
    keep = kept(order_ref[...])
    for c in range(FIELDS):
        coarse = jnp.where(keep, state_ref[c], 0.0)
        rows = exact_dot(trace_ref[0 : 2 * QP, :], coarse)
        for f in range(2):
            first_ref[f, c * QP : (c + 1) * QP, :] = rows[f * QP : (f + 1) * QP, :HALF]
            last_ref[f, c * QP : (c + 1) * QP, :] = rows[f * QP : (f + 1) * QP, KE - HALF :]


def edges(order_row, state, trace):
    shape = jax.ShapeDtypeStruct((2, FIELDS * QP, HALF), jnp.float32)
    return pl.pallas_call(
        edge_kernel,
        out_shape=(shape, shape),
        compiler_params=pltpu.CompilerParams(vmem_limit_bytes=VMEM),
        name="edges",
    )(order_row, state, trace)


def indicator_kernel(
    device_ref,
    order_ref,
    near_ref,
    state_ref,
    adjoint_ref,
    jacobian_ref,
    enrich_ref,
    volume_ref,
    trace_ref,
    lift_ref,
    lift_edge_ref,
    top_ref,
    own_ref,
    rows_ref,
    edge_ref,
    picks_ref,
    traces_ref,
    jump_ref,
    flux_ref,
    coarse_ref,
):
    order_row = order_ref[...]
    keep = kept(order_row)
    start = device_ref[0] * KE
    for c in range(FIELDS):
        coarse = jnp.where(keep, state_ref[c], 0.0)
        coarse_ref[c] = coarse
        rows = exact_dot(trace_ref[...], coarse)
        for f in range(6):
            traces_ref[f, c * QP : (c + 1) * QP, :] = rows[f * QP : (f + 1) * QP, :]
    for f in range(6):
        near = near_ref[f : f + 1, :]
        local = jnp.where(near >= 0, near - start, -(1 << 20))
        at = lax.broadcasted_iota(jnp.int32, (KE, KE), 0)
        own = jnp.where(at == local, 1.0, 0.0).astype(jnp.bfloat16)
        jump_ref[f] = dot_exact(traces_ref[f ^ 1], own) - traces_ref[f]
        if f < 2:
            place = jnp.where(at < HALF, at - HALF, at + HALF)
            picks_ref[f] = jnp.where(place == local, 1.0, 0.0).astype(jnp.bfloat16)
    top = top_ref[...]
    enrich = jnp.where(
        top == 3.0,
        enrich_ref[0],
        jnp.where(top == 4.0, enrich_ref[1], jnp.where(top == 5.0, enrich_ref[2], 0.0)),
    )
    enrich_parts = parts(enrich)
    rows_ref[...] = jnp.zeros(rows_ref.shape, jnp.bfloat16)
    rows_ref[0:RICH, 0:MODES] = enrich_parts[0]
    rows_ref[0:RICH, 128 : 128 + MODES] = enrich_parts[0]
    rows_ref[RICH:, 0:MODES] = enrich_parts[1]
    volume_parts = parts(volume_ref[...])
    new_mask = top == order_row.astype(jnp.float32) + 1.0
    total = jnp.zeros((RICH, KE), jnp.float32)
    for c in range(FIELDS):
        factors = jacobian_ref[c]
        weighted = factors[0:1, :] * coarse_ref[0]
        for h in range(1, FIELDS):
            weighted = weighted + factors[h : h + 1, :] * coarse_ref[h]
        for f in range(6):
            flux = factors[0:1, :] * jump_ref[f, 0:QP, :]
            for h in range(1, FIELDS):
                flux = flux + factors[h : h + 1, :] * jump_ref[f, h * QP : (h + 1) * QP, :]
            flux_ref[f * QP : (f + 1) * QP, :] = flux
        residual = dot_three(volume_parts, weighted) + exact_dot(lift_ref[...], flux_ref[...])
        new = dot_three(enrich_parts, jnp.where(keep, adjoint_ref[c], 0.0))
        new = jnp.where(new_mask, new, 0.0)
        total = total + new * residual
        lifted = exact_dot(lift_edge_ref[...], new)
        for f in range(2):
            for h in range(FIELDS):
                term = factors[h : h + 1, :] * lifted[f * QP : (f + 1) * QP, :]
                rows = slice(h * QP, (h + 1) * QP)
                edge_ref[f, rows, :] = term if c == 0 else edge_ref[f, rows, :] + term
    own_ref[...] = jnp.sum(total, axis=0, keepdims=True)


def own_indicators(device, order_row, near, state, adjoint, jacobian, enrich, volume):
    space = pl.BlockSpec(memory_space=pltpu.VMEM)
    return pl.pallas_call(
        indicator_kernel,
        in_specs=[pl.BlockSpec(memory_space=pltpu.SMEM)] + [space] * 11,
        out_specs=(space,) * 4,
        out_shape=(
            pltpu.HBM((1, KE), jnp.float32),
            pltpu.HBM((2 * RICH, 256), jnp.bfloat16),
            pltpu.HBM((2, FIELDS * QP, KE), jnp.float32),
            pltpu.HBM((2, KE, KE), jnp.bfloat16),
        ),
        scratch_shapes=[
            pltpu.VMEM((6, FIELDS * QP, KE), jnp.float32),
            pltpu.VMEM((6, FIELDS * QP, KE), jnp.float32),
            pltpu.VMEM((6 * QP, KE), jnp.float32),
            pltpu.VMEM((FIELDS, MODES, KE), jnp.float32),
        ],
        compiler_params=pltpu.CompilerParams(vmem_limit_bytes=VMEM),
        name="own_indicators",
    )(
        device,
        order_row,
        near,
        state,
        adjoint,
        jacobian,
        enrich,
        volume,
        jnp.asarray(TRACE, jnp.bfloat16),
        jnp.asarray(LIFT, jnp.bfloat16),
        jnp.asarray(LIFT[:, : 2 * QP].T, jnp.bfloat16),
        jnp.asarray(RICH_TOP),
    )


def unpack_kernel(
    in_ref,
    rows_hbm,
    own_hbm,
    edge_hbm,
    picks_hbm,
    before_hbm,
    after_hbm,
    state_hbm,
    adjoint_hbm,
    ids_hbm,
    orders_hbm,
    indicator_hbm,
    rows_ref,
    own_ref,
    edge_ref,
    picks_ref,
    halo_ref,
    state_ref,
    adjoint_ref,
    ids_ref,
    orders_ref,
    indicator_ref,
    in_sems,
    out_sems,
):
    loads = [
        pltpu.make_async_copy(rows_hbm, rows_ref, in_sems.at[0]),
        pltpu.make_async_copy(own_hbm, own_ref, in_sems.at[1]),
        pltpu.make_async_copy(edge_hbm, edge_ref, in_sems.at[2]),
        pltpu.make_async_copy(picks_hbm, picks_ref, in_sems.at[3]),
        pltpu.make_async_copy(before_hbm, halo_ref.at[0], in_sems.at[4]),
        pltpu.make_async_copy(after_hbm, halo_ref.at[1], in_sems.at[5]),
    ]
    for copy in loads:
        copy.start()
    slots = ND * CAP
    n = lax.broadcasted_iota(jnp.int32, (RICH, 256), 0)
    i = (n * 57) >> 11
    rest = n - i * 36
    j = (rest * 43) >> 8
    k = rest - j * 6
    top = jnp.maximum(jnp.maximum(i, j), k)
    m = lax.broadcasted_iota(jnp.int32, (RICH, 256), 1) & 127
    embed = jnp.where((top < 5) & (m == i * 25 + j * 5 + k), 1.0, 0.0).astype(jnp.bfloat16)
    m = lax.broadcasted_iota(jnp.int32, (128, 256), 1) & 127
    eye = jnp.where(m == lax.broadcasted_iota(jnp.int32, (128, 256), 0), 1.0, 0.0)
    eye = eye.astype(jnp.bfloat16)
    top = jnp.concatenate([top, top], axis=1)
    upper = lax.broadcasted_iota(jnp.int32, (ND // 2, 8, 128), 1) >= CAP
    stores = []

    def store(source, target):
        copy = pltpu.make_async_copy(source, target, out_sems.at[len(stores)])
        copy.start()
        stores.append(copy)

    def doubled(x):
        high, low = parts(x.reshape(slots, 128))
        return jnp.concatenate([high, low], axis=1)

    for t in range(FIELDS):
        block = in_ref[:, 8 * t : 8 * t + 8, :].reshape(ND // 2, 2, 8, 128)
        even, odd = block[:, 0], block[:, 1]
        moved = dot_nt(eye, doubled(jnp.where(upper, pltpu.roll(odd, CAP, 1), even)))
        state_ref[t] = moved[0:MODES, :]
        store(state_ref.at[t], state_hbm.at[t])
        if t == 0:
            id_row = moved[125:126, :].astype(jnp.int32)
            order_row = moved[126:127, :].astype(jnp.int32)
            new_mask = top == order_row + 1
            first = (lax.broadcasted_iota(jnp.int32, (1, slots), 1) >> 2) * KE
            ids_ref[...] = jnp.where(id_row > 0, first + id_row - 1, -1)
            orders_ref[...] = order_row
            loads[0].wait()
        adjoint = doubled(jnp.where(upper, odd, pltpu.roll(even, CAP, 1)))
        new = dot_nt(rows_ref[0:RICH, :], adjoint) + dot_nt(
            rows_ref[RICH:, 0:128], adjoint[:, 0:128]
        )
        adjoint_ref[t] = dot_nt(embed, adjoint) + jnp.where(new_mask, new, 0.0)
        store(adjoint_ref.at[t], adjoint_hbm.at[t])
        if t == 0:
            store(ids_ref, ids_hbm)
            store(orders_ref, orders_hbm)
    for copy in loads[1:]:
        copy.wait()
    total = own_ref[...]
    for f in range(2):
        halo = jnp.concatenate([halo_ref[0, f ^ 1], halo_ref[1, f ^ 1]], axis=1)
        found = dot_exact(halo, picks_ref[f])
        total = total + jnp.sum(found * edge_ref[f], axis=0, keepdims=True)
    indicator_ref[...] = jnp.abs(total) * (1.0 / 216.0)
    store(indicator_ref, indicator_hbm)
    for copy in stores:
        copy.wait()


def unpack(received, rows, own, edge, picks, before, after):
    slots = ND * CAP
    far = pl.BlockSpec(memory_space=pltpu.HBM)
    shapes = (
        ((FIELDS, MODES, slots), jnp.float32),
        ((FIELDS, RICH, slots), jnp.float32),
        ((1, slots), jnp.int32),
        ((1, slots), jnp.int32),
        ((1, KE), jnp.float32),
    )
    return pl.pallas_call(
        unpack_kernel,
        in_specs=[pl.BlockSpec(memory_space=pltpu.VMEM)] + [far] * 6,
        out_specs=(far,) * 5,
        out_shape=tuple(pltpu.HBM(*a) for a in shapes),
        scratch_shapes=[
            pltpu.VMEM((2 * RICH, 256), jnp.bfloat16),
            pltpu.VMEM((1, KE), jnp.float32),
            pltpu.VMEM((2, FIELDS * QP, KE), jnp.float32),
            pltpu.VMEM((2, KE, KE), jnp.bfloat16),
            pltpu.VMEM((2, 2, FIELDS * QP, HALF), jnp.float32),
        ]
        + [pltpu.VMEM(*a) for a in shapes]
        + [pltpu.SemaphoreType.DMA((6,)), pltpu.SemaphoreType.DMA((2 * FIELDS + 3,))],
        compiler_params=pltpu.CompilerParams(vmem_limit_bytes=VMEM),
        name="unpack",
    )(received, hbm(rows), hbm(own), hbm(edge), hbm(picks), hbm(before), hbm(after))


def body(state, adjoint, order, neighbours, owner, jacobian, enrich, volume):
    device = lax.axis_index("dom")
    order_row = order.reshape(1, KE)
    message = pack(order_row, owner.reshape(1, KE), state, adjoint)
    received = lax.all_to_all(message, "dom", split_axis=0, concat_axis=0, tiled=True)
    first, last = edges(order_row, state, jnp.asarray(TRACE, jnp.bfloat16))
    up = [(i, i + 1) for i in range(ND - 1)]
    down = [(i + 1, i) for i in range(ND - 1)]
    before = lax.ppermute(last, "dom", up)
    after = lax.ppermute(first, "dom", down)
    own, rows, edge, picks = own_indicators(
        device.reshape(1), order_row, neighbours, state, adjoint, jacobian, enrich, volume
    )
    moved_state, moved_adjoint, ids, orders, indicator = unpack(
        received, rows, own, edge, picks, before, after
    )
    return (
        indicator.reshape(KE),
        moved_state,
        moved_adjoint,
        ids.reshape(ND * CAP),
        orders.reshape(ND * CAP),
    )


def solution(mesh):
    wide = P(None, None, "dom")
    in_specs = (wide, wide, P("dom"), P(None, "dom"), P("dom", None), wide, P(), P())
    out_specs = (P("dom"), wide, wide, P("dom"), P("dom"))
    return jax.shard_map(body, mesh=mesh, in_specs=in_specs, out_specs=out_specs, check_vma=False)
```

time: 73.5 us -> 57.4 us (0.78)
  waiting for transfers between devices: 26.1 us -> 17.1 us
  local copies, waits for them, and re-layouts: 12.6 us -> 5.22 us
    ppermute x1, waiting for transfers between devices: 26.1 us -> 17.1 us  [body(): before = lax.ppermute(last, 'dom', up)]
    unnamed x38 -> x22, local copies, waits for them, and re-layouts: 12.6 us -> 5.22 us
  transfers between devices with their start and end apart: 3 -> 3, of which waited for: 1 -> 1; matrix products, arithmetic and copies ran while one was open for 0% -> 0% of each run, Pallas kernels for 7% -> 8%
where the time goes in v2:
time: 57.4 us; the launch traced here: 56.7 us
  starting transfers between devices  20.3 us (35%)
  waiting for transfers between devices  17.1 us (30%)
  Pallas kernels  13.4 us (23%)
  local copies, waits for them, and re-layouts  5.22 us (9%)
  between operations  0.76 us (1%)
    ppermute x1, waiting for transfers between devices, body(): before = lax.ppermute(last, 'dom', up)  17.1 us
    all_to_all x1, starting transfers between devices, body(): lax.all_to_all(message, 'dom', split_axis=0, concat_axis=0, tiled=True)  10.5 us
    ppermute x1, starting transfers between devices, body(): after = lax.ppermute(first, 'dom', down)  7.73 us
    unnamed x22, local copies, waits for them, and re-layouts  5.22 us
    pallas_call x1, Pallas kernels, pack(): pl.pallas_call(pack_kernel, in_specs=[far] * 4, out_specs=far, out_shape=...  5.06 us
    pallas_call x1, Pallas kernels, own_indicators(): pl.pallas_call(indicator_kernel, in_specs=[pl.BlockSpec(memory_space=pltp...  3.75 us
    pallas_call x1, Pallas kernels, unpack(): pl.pallas_call(unpack_kernel, in_specs=[pl.BlockSpec(memory_space=pltpu.V...  3.48 us
    ppermute x1, starting transfers between devices, body(): before = lax.ppermute(last, 'dom', up)  2.05 us
  transfers between devices with their start and end apart: 3, of which 1 were waited for; matrix products, arithmetic and copies ran while one was open for 0% of the time, Pallas kernels for 8%

profile of v2, /device:TPU:2, one launch (start us, length us, event | category | flops | bytes accessed | tf_op | source)
XLA Modules:
  0.0 56.7 jit_solution(16739703005258729812)
XLA Ops:
  0.6 5.1 %pack.1 = f32[128,40,128]{2,1,0:T(8,128)} custom-call(s32[1,256]{1,0:T(1,128)} %bitcast.6, s32[1,256]{1,0:T(1,128)} %bitcast.9, f32[5,125,256]{2,1,0:T(8,128)} %state_ref.3, f32[5,125,256]{2,1,0:T(8,128)} %adjoint_ref.1), custom_call_target="tpu_custom_call" | custom-call | tf_op jit(solution)/shard_map/pack/pallas_call | solution.py:159
  5.7 0.0 copy-start
  5.7 0.0 copy-start.3
  5.7 0.0 copy-start.9
  5.7 0.0 copy-start.4
  5.8 0.0 copy-start.5
  5.8 10.5 %all-to-all-start = ((f32[128,40,128]{2,1,0:T(8,128)}), f32[128,40,128]{2,1,0:T(8,128)S(1)}, u32[]{:S(2)}, u32[]{:S(2)}) async-start(f32[128,40,128]{2,1,0:T(8,128)} %pack.1), calls=%async_computation | async-start | bytes 5242880 | tf_op jit(solution)/shard_map/all_to_all | solution.py:442
  16.3 0.0 copy-done
  16.3 0.0 copy-done.3
  16.3 1.1 %edges.1 = (f32[2,160,128]{2,1,0:T(8,128)}, f32[2,160,128]{2,1,0:T(8,128)}) custom-call(s32[1,256]{1,0:T(1,128)S(1)} %bitcast.7, f32[5,125,256]{2,1,0:T(8,128)S(1)} %copy-done, bf16[192,125]{1,0:T(8,128)(2,1)S(1)} %copy-done.3), custom_call_target="tpu_custom_call" | custom-call | tf_op jit(solution)/shard_map/edges/pallas_call | solution.py:191
  17.4 2.0 %collective-permute-start = (f32[2,160,128]{2,1,0:T(8,128)}, f32[2,160,128]{2,1,0:T(8,128)}, u32[]{:S(2)}, u32[]{:S(2)}) collective-permute-start(f32[2,160,128]{2,1,0:T(8,128)} %get-tuple-element.20), channel_id=1, source_target_pairs={{0,1},{1,2},{2,3},{3,4},{4,5},{5,6},{6,7},{7,8},{8,9},{9,10},{10,1... | collective-permute-start | bytes 491528 | tf_op jit(solution)/shard_map/ppermute | solution.py:446
  19.5 7.7 %collective-permute-start.1 = (f32[2,160,128]{2,1,0:T(8,128)}, f32[2,160,128]{2,1,0:T(8,128)}, u32[]{:S(2)}, u32[]{:S(2)}) collective-permute-start(f32[2,160,128]{2,1,0:T(8,128)} %get-tuple-element.21), channel_id=1, source_target_pairs={{1,0},{2,1},{3,2},{4,3},{5,4},{6,5},{7,6},{8,7},{9,8},{10,9},{11,1... | collective-permute-start | bytes 491528 | tf_op jit(solution)/shard_map/ppermute | solution.py:447
  27.2 0.0 copy-start.1
  27.2 1.1 %copy-done.1 = f32[5,125,256]{2,1,0:T(8,128)S(1)} copy-done((f32[5,125,256]{2,1,0:T(8,128)S(1)}, f32[5,125,256]{2,1,0:T(8,128)}, u32[]{:S(2)}) %copy-start.1) | copy-done | bytes 640024
  28.3 1.0 %copy-done.2 = f32[3,216,125]{2,1,0:T(8,128)S(1)} copy-done((f32[3,216,125]{2,1,0:T(8,128)S(1)}, f32[3,216,125]{2,1,0:T(8,128)}, u32[]{:S(2)}) %copy-start.2) | copy-done | bytes 324024
  29.3 0.9 %copy-done.6 = bf16[216,192]{1,0:T(8,128)(2,1)S(1)} copy-done((bf16[216,192]{1,0:T(8,128)(2,1)S(1)}, bf16[216,192]{1,0:T(8,128)(2,1)}, u32[]{:S(2)}) %copy-start.6) | copy-done | bytes 82968
  30.2 0.8 %copy-done.7 = f32[5,5,256]{2,1,0:T(8,128)S(1)} copy-done((f32[5,5,256]{2,1,0:T(8,128)S(1)}, f32[5,5,256]{2,1,0:T(8,128)}, u32[]{:S(2)}) %copy-start.7) | copy-done | bytes 25624
  31.0 0.8 %copy-done.8 = bf16[64,216]{1,0:T(8,128)(2,1)S(1)} copy-done((bf16[64,216]{1,0:T(8,128)(2,1)S(1)}, bf16[64,216]{1,0:T(8,128)(2,1)}, u32[]{:S(2)}) %copy-start.8) | copy-done | bytes 27672
  31.7 0.7 %copy-done.10 = s32[6,256]{1,0:T(8,128)S(1)} copy-done((s32[6,256]{1,0:T(8,128)S(1)}, s32[6,256]{1,0:T(8,128)}, u32[]{:S(2)}) %copy-start.10) | copy-done | bytes 6168
  32.4 3.8 %own_indicators.1 = (f32[1,256]{1,0:T(1,128)}, bf16[432,256]{1,0:T(8,128)(2,1)}, f32[2,160,256]{2,1,0:T(8,128)}, bf16[2,256,256]{2,1,0:T(8,128)(2,1)}) custom-call(s32[1]{0:T(128)} %bitcast.2.device_ref, s32[1,256]{1,0:T(1,128)S(1)} %bitcast.8, s32[6,256]{1,0:T(8,128)S(1)} %copy-done.10, f32[5,125,256]{2,1,0:T(8,128)S(1)} %copy-done, ...), custom_call_target="tpu_custom_call" | custom-call | tf_op jit(solution)/shard_map/own_indicators/pallas_call | solution.py:278
  36.2 17.1 %collective-permute-done.before_hbm = f32[2,160,128]{2,1,0:T(8,128)} collective-permute-done((f32[2,160,128]{2,1,0:T(8,128)}, f32[2,160,128]{2,1,0:T(8,128)}, u32[]{:S(2)}, u32[]{:S(2)}) %collective-permute-start) | collective-permute-done | bytes 163872 | tf_op jit(solution)/shard_map/ppermute | solution.py:446
  53.2 0.0 collective-permute-done.1.after_hbm
  53.3 0.0 all-to-all-done.in_ref
  53.3 3.5 %unpack.1 = (f32[5,125,512]{2,1,0:T(8,128)}, f32[5,216,512]{2,1,0:T(8,128)}, s32[1,512]{1,0:T(1,128)}, s32[1,512]{1,0:T(1,128)}, f32[1,256]{1,0:T(1,128)}) custom-call(f32[128,40,128]{2,1,0:T(8,128)S(1)} %all-to-all-done.in_ref, bf16[432,256]{1,0:T(8,128)(2,1)} %get-tuple-element.16.rows_hbm, f32[1,256]{1,0:T(1,128)} %get-tuple-element.17.own_hbm, ...), custom_call_target="tpu_custom_call" | custom-call | tf_op jit(solution)/shard_map/unpack/pallas_call | solution.py:419
  (8 shorter events, 0.0 us)
Async XLA Ops:
  5.7 10.6 %copy-start = (f32[5,125,256]{2,1,0:T(8,128)S(1)}, f32[5,125,256]{2,1,0:T(8,128)}, u32[]{:S(2)}) copy-start(f32[5,125,256]{2,1,0:T(8,128)} %state_ref.3) | copy-start | bytes 1920004
  5.7 10.6 %copy-start.3 = (bf16[192,125]{1,0:T(8,128)(2,1)S(1)}, bf16[192,125]{1,0:T(8,128)(2,1)}, u32[]{:S(2)}) copy-start(bf16[192,125]{1,0:T(8,128)(2,1)} %constant.12.clone.trace_ref) | copy-start | bytes 144004
  5.7 10.6 %copy-start.9 = (s32[256]{0:T(256)S(1)}, s32[256]{0:T(256)}, u32[]{:S(2)}) copy-start(s32[256]{0:T(256)} %param.15) | copy-start | bytes 3076
  5.7 21.5 %copy-start.4 = (f32[216,125]{1,0:T(8,128)S(1)}, f32[216,125]{1,0:T(8,128)}, u32[]{:S(2)}) copy-start(f32[216,125]{1,0:T(8,128)} %volume_ref.1) | copy-start | bytes 324004
  5.8 21.5 %copy-start.5 = (f32[216,1]{1,0:T(8,128)S(1)}, f32[216,1]{1,0:T(8,128)}, u32[]{:S(2)}) copy-start(f32[216,1]{1,0:T(8,128)} %constant.15.clone.top_ref) | copy-start | bytes 2596
  5.8 47.5 %all-to-all-start = ((f32[128,40,128]{2,1,0:T(8,128)}), f32[128,40,128]{2,1,0:T(8,128)S(1)}, u32[]{:S(2)}, u32[]{:S(2)}) async-start(f32[128,40,128]{2,1,0:T(8,128)} %pack.1), calls=%async_computation | async-start | bytes 5242880 | tf_op jit(solution)/shard_map/all_to_all | solution.py:442
  17.4 35.9 %collective-permute-start = (f32[2,160,128]{2,1,0:T(8,128)}, f32[2,160,128]{2,1,0:T(8,128)}, u32[]{:S(2)}, u32[]{:S(2)}) collective-permute-start(f32[2,160,128]{2,1,0:T(8,128)} %get-tuple-element.20), channel_id=1, source_target_pairs={{0,1},{1,2},{2,3},{3,4},{4,5},{5,6},{6,7},{7,8},{8,9},{9,10},{10,1... | collective-permute-start | bytes 491528 | tf_op jit(solution)/shard_map/ppermute | solution.py:446
  19.5 33.8 %collective-permute-start.1 = (f32[2,160,128]{2,1,0:T(8,128)}, f32[2,160,128]{2,1,0:T(8,128)}, u32[]{:S(2)}, u32[]{:S(2)}) collective-permute-start(f32[2,160,128]{2,1,0:T(8,128)} %get-tuple-element.21), channel_id=1, source_target_pairs={{1,0},{2,1},{3,2},{4,3},{5,4},{6,5},{7,6},{8,7},{9,8},{10,9},{11,1... | collective-permute-start | bytes 491528 | tf_op jit(solution)/shard_map/ppermute | solution.py:447
  27.2 1.1 %copy-start.1 = (f32[5,125,256]{2,1,0:T(8,128)S(1)}, f32[5,125,256]{2,1,0:T(8,128)}, u32[]{:S(2)}) copy-start(f32[5,125,256]{2,1,0:T(8,128)} %adjoint_ref.1) | copy-start | bytes 1920004
  28.3 1.0 %copy-start.2 = (f32[3,216,125]{2,1,0:T(8,128)S(1)}, f32[3,216,125]{2,1,0:T(8,128)}, u32[]{:S(2)}) copy-start(f32[3,216,125]{2,1,0:T(8,128)} %enrich_ref.1) | copy-start | bytes 972004
  29.3 0.9 %copy-start.6 = (bf16[216,192]{1,0:T(8,128)(2,1)S(1)}, bf16[216,192]{1,0:T(8,128)(2,1)}, u32[]{:S(2)}) copy-start(bf16[216,192]{1,0:T(8,128)(2,1)} %constant.13.clone.lift_ref) | copy-start | bytes 248836
  30.2 0.8 %copy-start.7 = (f32[5,5,256]{2,1,0:T(8,128)S(1)}, f32[5,5,256]{2,1,0:T(8,128)}, u32[]{:S(2)}) copy-start(f32[5,5,256]{2,1,0:T(8,128)} %jacobian_ref.1) | copy-start | bytes 76804
  31.0 0.8 %copy-start.8 = (bf16[64,216]{1,0:T(8,128)(2,1)S(1)}, bf16[64,216]{1,0:T(8,128)(2,1)}, u32[]{:S(2)}) copy-start(bf16[64,216]{1,0:T(8,128)(2,1)} %constant.14.clone.lift_edge_ref) | copy-start | bytes 82948
  31.7 0.7 %copy-start.10 = (s32[6,256]{1,0:T(8,128)S(1)}, s32[6,256]{1,0:T(8,128)}, u32[]{:S(2)}) copy-start(s32[6,256]{1,0:T(8,128)} %near_ref.1) | copy-start | bytes 18436

commit v3 on v2

--- a/solution.py
+++ b/solution.py
@@ -101,57 +101,62 @@
         pltpu.make_async_copy(owner_hbm, owner_ref, in_sems.at[1]),
     ]
     fields = [
-        (
-            pltpu.make_async_copy(state_hbm.at[t], state_ref.at[t], in_sems.at[2 + 2 * t]),
-            pltpu.make_async_copy(adjoint_hbm.at[t], adjoint_ref.at[t], in_sems.at[3 + 2 * t]),
-        )
-        for t in range(FIELDS)
+        pltpu.make_async_copy(state_hbm, state_ref, in_sems.at[2]),
+        pltpu.make_async_copy(adjoint_hbm, adjoint_ref, in_sems.at[3]),
     ]
     for copy in small:
         copy.start()
-    for pair in fields:
-        for copy in pair:
-            copy.start()
+    for copy in fields:
+        copy.start()
     before = lax.broadcasted_iota(jnp.int32, (KE, KE), 0) < lax.broadcasted_iota(
         jnp.int32, (KE, KE), 1
     )
     before = jnp.where(before, 1.0, 0.0).astype(jnp.bfloat16)
     local = lax.broadcasted_iota(jnp.int32, (1, KE), 1)
-    x_ref[125:126, :] = (local + 1).astype(jnp.float32)
-    x_ref[127:128, :] = jnp.zeros((1, KE), jnp.float32)
-    x_ref[253:256, :] = jnp.zeros((3, KE), jnp.float32)
+    for t in range(FIELDS):
+        x_ref[t, 125:126, :] = (local + 1).astype(jnp.float32)
+        x_ref[t, 127:128, :] = jnp.zeros((1, KE), jnp.float32)
+        x_ref[t, 253:256, :] = jnp.zeros((3, KE), jnp.float32)
     for copy in small:
         copy.wait()
     order_row = order_ref[...]
-    x_ref[126:127, :] = order_row.astype(jnp.float32)
+    for t in range(FIELDS):
+        x_ref[t, 126:127, :] = order_row.astype(jnp.float32)
     hits = owner_ref[...] == lax.broadcasted_iota(jnp.int32, (ND, KE), 0)
     count = dot(jnp.where(hits, 1.0, 0.0).astype(jnp.bfloat16), before)
-    sel = jnp.concatenate(
-        [
-            jnp.where(hits & (count == float(r)), 1.0, 0.0).astype(jnp.bfloat16)
-            for r in range(CAP)
-        ],
-        axis=0,
-    )
+    rank = jnp.sum(jnp.where(hits, count, 0.0), axis=0, keepdims=True).astype(jnp.int32)
+    slot = owner_ref[...] * CAP + rank
+    sel = jnp.where(slot == lax.broadcasted_iota(jnp.int32, (CAP * ND, KE), 0), 1.0, 0.0)
+    sel = sel.astype(jnp.bfloat16)
+    upper = lax.broadcasted_iota(jnp.int32, (ND // 2, 8, 128), 1) >= CAP
     keep = kept(order_row)
     sends = []
+
+    def prepare(t):
+        x_ref[t, 0:MODES, :] = jnp.where(keep, state_ref[t], 0.0)
+        x_ref[t, 128 : 128 + MODES, :] = jnp.where(keep, adjoint_ref[t], 0.0)
+        return parts(x_ref[t])
+
+    def gather(pair):
+        return dot_nt(sel, pair[0]) + dot_nt(sel, pair[1])
+
+    def send(t, rows):
+        low_rows = rows[:, 0:128].reshape(ND // 2, 8, 128)
+        high_rows = rows[:, 128:256].reshape(ND // 2, 8, 128)
+        out_ref[t, :, 0] = jnp.where(upper, pltpu.roll(high_rows, CAP, 1), low_rows)
+        out_ref[t, :, 1] = jnp.where(upper, high_rows, pltpu.roll(low_rows, CAP, 1))
+        copy = pltpu.make_async_copy(
+            out_ref.at[t], out_hbm.at[:, :, pl.ds(8 * t, 8), :], out_sems.at[t]
+        )
+        copy.start()
+        sends.append(copy)
+
+    for copy in fields:
+        copy.wait()
     for t in range(FIELDS):
-        for copy in fields[t]:
-            copy.wait()
-        x_ref[0:MODES, :] = jnp.where(keep, state_ref[t], 0.0)
-        x_ref[128 : 128 + MODES, :] = jnp.where(keep, adjoint_ref[t], 0.0)
-        high, low = parts(x_ref[...])
-        rows = dot_nt(sel, high) + dot_nt(sel, low)
-        for r in range(CAP):
-            out_ref[t, :, r, :] = rows[r * ND : (r + 1) * ND, 0:128]
-            out_ref[t, :, CAP + r, :] = rows[r * ND : (r + 1) * ND, 128:256]
-        send = pltpu.make_async_copy(
-            out_ref.at[t], out_hbm.at[:, pl.ds(8 * t, 8), :], out_sems.at[t]
-        )
-        send.start()
-        sends.append(send)
-    for send in sends:
-        send.wait()
+        send(t, gather(prepare(t)))
+    for copy in sends:
+        copy.wait()
 
 
 def pack(order_row, owner_row, state, adjoint):
@@ -160,20 +165,20 @@
         pack_kernel,
         in_specs=[far] * 4,
         out_specs=far,
-        out_shape=pltpu.HBM((ND, 8 * FIELDS, 128), jnp.float32),
+        out_shape=pltpu.HBM((ND // 2, 2, 8 * FIELDS, 128), jnp.float32),
         scratch_shapes=[
             pltpu.VMEM((1, KE), jnp.int32),
             pltpu.VMEM((1, KE), jnp.int32),
             pltpu.VMEM((FIELDS, MODES, KE), jnp.float32),
             pltpu.VMEM((FIELDS, MODES, KE), jnp.float32),
-            pltpu.VMEM((256, KE), jnp.float32),
-            pltpu.VMEM((FIELDS, ND, 8, 128), jnp.float32),
-            pltpu.SemaphoreType.DMA((2 + 2 * FIELDS,)),
+            pltpu.VMEM((FIELDS, 256, KE), jnp.float32),
+            pltpu.VMEM((FIELDS, ND // 2, 2, 8, 128), jnp.float32),
+            pltpu.SemaphoreType.DMA((4,)),
             pltpu.SemaphoreType.DMA((FIELDS,)),
         ],
         compiler_params=pltpu.CompilerParams(vmem_limit_bytes=VMEM),
         name="pack",
-    )(hbm(order_row), hbm(owner_row), hbm(state), hbm(adjoint))
+    )(hbm(order_row), hbm(owner_row), hbm(state), hbm(adjoint)).reshape(ND, 8 * FIELDS, 128)
 
 
 def edge_kernel(order_ref, state_ref, trace_ref, first_ref, last_ref):
@@ -336,7 +341,7 @@
     out_sems,
 ):
     loads = [
-        pltpu.make_async_copy(rows_hbm, rows_ref, in_sems.at[0]),
+        pltpu.make_async_copy(rows_hbm, rows_ref.at[pl.ds(0, 2 * RICH)], in_sems.at[0]),
         pltpu.make_async_copy(own_hbm, own_ref, in_sems.at[1]),
         pltpu.make_async_copy(edge_hbm, edge_ref, in_sems.at[2]),
         pltpu.make_async_copy(picks_hbm, picks_ref, in_sems.at[3]),
@@ -354,6 +359,7 @@
     top = jnp.maximum(jnp.maximum(i, j), k)
     m = lax.broadcasted_iota(jnp.int32, (RICH, 256), 1) & 127
     embed = jnp.where((top < 5) & (m == i * 25 + j * 5 + k), 1.0, 0.0).astype(jnp.bfloat16)
+    rows_ref[2 * RICH :, :] = embed
     m = lax.broadcasted_iota(jnp.int32, (128, 256), 1) & 127
     eye = jnp.where(m == lax.broadcasted_iota(jnp.int32, (128, 256), 0), 1.0, 0.0)
     eye = eye.astype(jnp.bfloat16)
@@ -370,38 +376,55 @@
         high, low = parts(x.reshape(slots, 128))
         return jnp.concatenate([high, low], axis=1)
 
-    for t in range(FIELDS):
+    def finish():
+        for copy in loads[1:]:
+            copy.wait()
+        total = own_ref[...]
+        for f in range(2):
+            halo = jnp.concatenate([halo_ref[0, f ^ 1], halo_ref[1, f ^ 1]], axis=1)
+            found = dot_exact(halo, picks_ref[f])
+            total = total + jnp.sum(found * edge_ref[f], axis=0, keepdims=True)
+        indicator_ref[...] = jnp.abs(total) * (1.0 / 216.0)
+
+    def split(t):
         block = in_ref[:, 8 * t : 8 * t + 8, :].reshape(ND // 2, 2, 8, 128)
         even, odd = block[:, 0], block[:, 1]
-        moved = dot_nt(eye, doubled(jnp.where(upper, pltpu.roll(odd, CAP, 1), even)))
+        state = jnp.where(upper, pltpu.roll(odd, CAP, 1), even)
+        return state, jnp.where(upper, odd, pltpu.roll(even, CAP, 1))
+
+    def put_state(t, state):
+        moved = state.reshape(slots, 128).T
         state_ref[t] = moved[0:MODES, :]
-        store(state_ref.at[t], state_hbm.at[t])
+        return moved
+
+    def put_adjoint(t, both, new_mask):
+        new = both[0:RICH] + both[RICH : 2 * RICH]
+        adjoint_ref[t] = both[2 * RICH :] + jnp.where(new_mask, new, 0.0)
+
+    def labels(moved):
+        id_row = moved[125:126, :].astype(jnp.int32)
+        order_row = moved[126:127, :].astype(jnp.int32)
+        first = (lax.broadcasted_iota(jnp.int32, (1, slots), 1) >> 2) * KE
+        ids_ref[...] = jnp.where(id_row > 0, first + id_row - 1, -1)
+        orders_ref[...] = order_row
+        return top == order_row + 1
+
+    moves = []
+    for t in range(FIELDS):
+        state, adjoint = split(t)
+        moved = put_state(t, state)
         if t == 0:
-            id_row = moved[125:126, :].astype(jnp.int32)
-            order_row = moved[126:127, :].astype(jnp.int32)
-            new_mask = top == order_row + 1
-            first = (lax.broadcasted_iota(jnp.int32, (1, slots), 1) >> 2) * KE
-            ids_ref[...] = jnp.where(id_row > 0, first + id_row - 1, -1)
-            orders_ref[...] = order_row
-            loads[0].wait()
-        adjoint = doubled(jnp.where(upper, odd, pltpu.roll(even, CAP, 1)))
-        new = dot_nt(rows_ref[0:RICH, :], adjoint) + dot_nt(
-            rows_ref[RICH:, 0:128], adjoint[:, 0:128]
-        )
-        adjoint_ref[t] = dot_nt(embed, adjoint) + jnp.where(new_mask, new, 0.0)
-        store(adjoint_ref.at[t], adjoint_hbm.at[t])
-        if t == 0:
+            new_mask = labels(moved)
+    store(state_ref, state_hbm)
+    loads[0].wait()
+    for t in range(FIELDS):
+        put_adjoint(t, dot_nt(rows_ref[...], doubled(split(t)[1])), new_mask)
+        if t == 2:
+            finish()
+            store(indicator_ref, indicator_hbm)
             store(ids_ref, ids_hbm)
             store(orders_ref, orders_hbm)
-    for copy in loads[1:]:
-        copy.wait()
-    total = own_ref[...]
-    for f in range(2):
-        halo = jnp.concatenate([halo_ref[0, f ^ 1], halo_ref[1, f ^ 1]], axis=1)
-        found = dot_exact(halo, picks_ref[f])
-        total = total + jnp.sum(found * edge_ref[f], axis=0, keepdims=True)
-    indicator_ref[...] = jnp.abs(total) * (1.0 / 216.0)
-    store(indicator_ref, indicator_hbm)
+        store(adjoint_ref.at[t], adjoint_hbm.at[t])
     for copy in stores:
         copy.wait()
 
@@ -422,7 +445,7 @@
         out_specs=(far,) * 5,
         out_shape=tuple(pltpu.HBM(*a) for a in shapes),
         scratch_shapes=[
-            pltpu.VMEM((2 * RICH, 256), jnp.bfloat16),
+            pltpu.VMEM((3 * RICH, 256), jnp.bfloat16),
             pltpu.VMEM((1, KE), jnp.float32),
             pltpu.VMEM((2, FIELDS * QP, KE), jnp.float32),
             pltpu.VMEM((2, KE, KE), jnp.bfloat16),

time: 57.4 us -> 55.7 us (0.970)
  Pallas kernels: 13.4 us -> 11.6 us
    pallas_call x1, Pallas kernels: 5.06 us -> 3.51 us  [pack(): pl.pallas_call(pack_kernel, in_specs=[far] * 4, out_specs=far, out_shape=...]
  transfers between devices with their start and end apart: 3 -> 3, of which waited for: 1 -> 1; matrix products, arithmetic and copies ran while one was open for 0% -> 0% of each run, Pallas kernels for 8% -> 9%
where the time goes in v3:
time: 55.7 us; the launch traced here: 55 us
  starting transfers between devices  20.3 us (36%)
  waiting for transfers between devices  17.1 us (31%)
  Pallas kernels  11.6 us (21%)
  local copies, waits for them, and re-layouts  5.22 us (9%)
  between operations  0.76 us (1%)
    ppermute x1, waiting for transfers between devices, body(): before = lax.ppermute(last, 'dom', up)  17.1 us
    all_to_all x1, starting transfers between devices, body(): lax.all_to_all(message, 'dom', split_axis=0, concat_axis=0, tiled=True)  10.5 us
    ppermute x1, starting transfers between devices, body(): after = lax.ppermute(first, 'dom', down)  7.73 us
    unnamed x22, local copies, waits for them, and re-layouts  5.22 us
    pallas_call x1, Pallas kernels, own_indicators(): pl.pallas_call(indicator_kernel, in_specs=[pl.BlockSpec(memory_space=pltp...  3.75 us
    pallas_call x1, Pallas kernels, pack(): pl.pallas_call(pack_kernel, in_specs=[far] * 4, out_specs=far, out_shape=...  3.51 us
    pallas_call x1, Pallas kernels, unpack(): pl.pallas_call(unpack_kernel, in_specs=[pl.BlockSpec(memory_space=pltpu.V...  3.27 us
    ppermute x1, starting transfers between devices, body(): before = lax.ppermute(last, 'dom', up)  2.05 us
  transfers between devices with their start and end apart: 3, of which 1 were waited for; matrix products, arithmetic and copies ran while one was open for 0% of the time, Pallas kernels for 9%

profile of v3, /device:TPU:2, one launch (start us, length us, event | category | flops | bytes accessed | tf_op | source)
XLA Modules:
  0.0 55.0 jit_solution(11175312084184288448)
XLA Ops:
  0.6 3.5 %pack.1 = f32[64,2,40,128]{3,2,1,0:T(8,128)} custom-call(s32[1,256]{1,0:T(1,128)} %bitcast.7, s32[1,256]{1,0:T(1,128)} %bitcast.11, f32[5,125,256]{2,1,0:T(8,128)} %state_ref.3, f32[5,125,256]{2,1,0:T(8,128)} %adjoint_ref.1), custom_call_target="tpu_custom_call" | custom-call | tf_op jit(solution)/shard_map/pack/pallas_call | solution.py:164
  4.1 0.0 copy-start
  4.2 0.0 copy-start.3
  4.2 0.0 copy-start.9
  4.2 0.0 copy-start.4
  4.2 0.0 copy-start.5
  4.2 10.5 %all-to-all-start = ((f32[128,40,128]{2,1,0:T(8,128)}), f32[128,40,128]{2,1,0:T(8,128)S(1)}, u32[]{:S(2)}, u32[]{:S(2)}) async-start(f32[128,40,128]{2,1,0:T(8,128)} %bitcast.10), calls=%async_computation | async-start | bytes 5242880 | tf_op jit(solution)/shard_map/all_to_all | solution.py:465
  14.8 1.1 %edges.1 = (f32[2,160,128]{2,1,0:T(8,128)}, f32[2,160,128]{2,1,0:T(8,128)}) custom-call(s32[1,256]{1,0:T(1,128)S(1)} %bitcast.8, f32[5,125,256]{2,1,0:T(8,128)S(1)} %copy-done, bf16[192,125]{1,0:T(8,128)(2,1)S(1)} %copy-done.3), custom_call_target="tpu_custom_call" | custom-call | tf_op jit(solution)/shard_map/edges/pallas_call | solution.py:196
  15.8 2.0 %collective-permute-start = (f32[2,160,128]{2,1,0:T(8,128)}, f32[2,160,128]{2,1,0:T(8,128)}, u32[]{:S(2)}, u32[]{:S(2)}) collective-permute-start(f32[2,160,128]{2,1,0:T(8,128)} %get-tuple-element.20), channel_id=1, source_target_pairs={{0,1},{1,2},{2,3},{3,4},{4,5},{5,6},{6,7},{7,8},{8,9},{9,10},{10,1... | collective-permute-start | bytes 491528 | tf_op jit(solution)/shard_map/ppermute | solution.py:469
  17.9 7.7 %collective-permute-start.1 = (f32[2,160,128]{2,1,0:T(8,128)}, f32[2,160,128]{2,1,0:T(8,128)}, u32[]{:S(2)}, u32[]{:S(2)}) collective-permute-start(f32[2,160,128]{2,1,0:T(8,128)} %get-tuple-element.21), channel_id=1, source_target_pairs={{1,0},{2,1},{3,2},{4,3},{5,4},{6,5},{7,6},{8,7},{9,8},{10,9},{11,1... | collective-permute-start | bytes 491528 | tf_op jit(solution)/shard_map/ppermute | solution.py:470
  25.6 0.0 copy-done.4
  25.6 0.0 copy-done.5
  25.6 0.0 copy-start.1
  25.7 1.1 %copy-done.1 = f32[5,125,256]{2,1,0:T(8,128)S(1)} copy-done((f32[5,125,256]{2,1,0:T(8,128)S(1)}, f32[5,125,256]{2,1,0:T(8,128)}, u32[]{:S(2)}) %copy-start.1) | copy-done | bytes 640024
  26.7 1.0 %copy-done.2 = f32[3,216,125]{2,1,0:T(8,128)S(1)} copy-done((f32[3,216,125]{2,1,0:T(8,128)S(1)}, f32[3,216,125]{2,1,0:T(8,128)}, u32[]{:S(2)}) %copy-start.2) | copy-done | bytes 324024
  27.7 0.9 %copy-done.6 = bf16[216,192]{1,0:T(8,128)(2,1)S(1)} copy-done((bf16[216,192]{1,0:T(8,128)(2,1)S(1)}, bf16[216,192]{1,0:T(8,128)(2,1)}, u32[]{:S(2)}) %copy-start.6) | copy-done | bytes 82968
  28.6 0.8 %copy-done.7 = f32[5,5,256]{2,1,0:T(8,128)S(1)} copy-done((f32[5,5,256]{2,1,0:T(8,128)S(1)}, f32[5,5,256]{2,1,0:T(8,128)}, u32[]{:S(2)}) %copy-start.7) | copy-done | bytes 25624
  29.4 0.8 %copy-done.8 = bf16[64,216]{1,0:T(8,128)(2,1)S(1)} copy-done((bf16[64,216]{1,0:T(8,128)(2,1)S(1)}, bf16[64,216]{1,0:T(8,128)(2,1)}, u32[]{:S(2)}) %copy-start.8) | copy-done | bytes 27672
  30.1 0.7 %copy-done.10 = s32[6,256]{1,0:T(8,128)S(1)} copy-done((s32[6,256]{1,0:T(8,128)S(1)}, s32[6,256]{1,0:T(8,128)}, u32[]{:S(2)}) %copy-start.10) | copy-done | bytes 6168
  30.8 3.8 %own_indicators.1 = (f32[1,256]{1,0:T(1,128)}, bf16[432,256]{1,0:T(8,128)(2,1)}, f32[2,160,256]{2,1,0:T(8,128)}, bf16[2,256,256]{2,1,0:T(8,128)(2,1)}) custom-call(s32[1]{0:T(128)} %bitcast.3.device_ref, s32[1,256]{1,0:T(1,128)S(1)} %bitcast.9, s32[6,256]{1,0:T(8,128)S(1)} %copy-done.10, f32[5,125,256]{2,1,0:T(8,128)S(1)} %copy-done, ...), custom_call_target="tpu_custom_call" | custom-call | tf_op jit(solution)/shard_map/own_indicators/pallas_call | solution.py:283
  34.6 17.1 %collective-permute-done.before_hbm = f32[2,160,128]{2,1,0:T(8,128)} collective-permute-done((f32[2,160,128]{2,1,0:T(8,128)}, f32[2,160,128]{2,1,0:T(8,128)}, u32[]{:S(2)}, u32[]{:S(2)}) %collective-permute-start) | collective-permute-done | bytes 163872 | tf_op jit(solution)/shard_map/ppermute | solution.py:469
  51.7 0.0 collective-permute-done.1.after_hbm
  51.7 0.0 all-to-all-done.in_ref
  51.7 3.3 %unpack.1 = (f32[5,125,512]{2,1,0:T(8,128)}, f32[5,216,512]{2,1,0:T(8,128)}, s32[1,512]{1,0:T(1,128)}, s32[1,512]{1,0:T(1,128)}, f32[1,256]{1,0:T(1,128)}) custom-call(f32[128,40,128]{2,1,0:T(8,128)S(1)} %all-to-all-done.in_ref, bf16[432,256]{1,0:T(8,128)(2,1)} %get-tuple-element.16.rows_hbm, f32[1,256]{1,0:T(1,128)} %get-tuple-element.17.own_hbm, ...), custom_call_target="tpu_custom_call" | custom-call | tf_op jit(solution)/shard_map/unpack/pallas_call | solution.py:442
  (8 shorter events, 0.0 us)
Async XLA Ops:
  4.1 10.6 %copy-start = (f32[5,125,256]{2,1,0:T(8,128)S(1)}, f32[5,125,256]{2,1,0:T(8,128)}, u32[]{:S(2)}) copy-start(f32[5,125,256]{2,1,0:T(8,128)} %state_ref.3) | copy-start | bytes 1920004
  4.2 10.6 %copy-start.3 = (bf16[192,125]{1,0:T(8,128)(2,1)S(1)}, bf16[192,125]{1,0:T(8,128)(2,1)}, u32[]{:S(2)}) copy-start(bf16[192,125]{1,0:T(8,128)(2,1)} %constant.12.clone.trace_ref) | copy-start | bytes 144004
  4.2 10.6 %copy-start.9 = (s32[256]{0:T(256)S(1)}, s32[256]{0:T(256)}, u32[]{:S(2)}) copy-start(s32[256]{0:T(256)} %param.15) | copy-start | bytes 3076
  4.2 21.4 %copy-start.4 = (f32[216,125]{1,0:T(8,128)S(1)}, f32[216,125]{1,0:T(8,128)}, u32[]{:S(2)}) copy-start(f32[216,125]{1,0:T(8,128)} %volume_ref.1) | copy-start | bytes 324004
  4.2 21.4 %copy-start.5 = (f32[216,1]{1,0:T(8,128)S(1)}, f32[216,1]{1,0:T(8,128)}, u32[]{:S(2)}) copy-start(f32[216,1]{1,0:T(8,128)} %constant.15.clone.top_ref) | copy-start | bytes 2596
  4.2 47.5 %all-to-all-start = ((f32[128,40,128]{2,1,0:T(8,128)}), f32[128,40,128]{2,1,0:T(8,128)S(1)}, u32[]{:S(2)}, u32[]{:S(2)}) async-start(f32[128,40,128]{2,1,0:T(8,128)} %bitcast.10), calls=%async_computation | async-start | bytes 5242880 | tf_op jit(solution)/shard_map/all_to_all | solution.py:465
  15.8 35.9 %collective-permute-start = (f32[2,160,128]{2,1,0:T(8,128)}, f32[2,160,128]{2,1,0:T(8,128)}, u32[]{:S(2)}, u32[]{:S(2)}) collective-permute-start(f32[2,160,128]{2,1,0:T(8,128)} %get-tuple-element.20), channel_id=1, source_target_pairs={{0,1},{1,2},{2,3},{3,4},{4,5},{5,6},{6,7},{7,8},{8,9},{9,10},{10,1... | collective-permute-start | bytes 491528 | tf_op jit(solution)/shard_map/ppermute | solution.py:469
  17.9 33.8 %collective-permute-start.1 = (f32[2,160,128]{2,1,0:T(8,128)}, f32[2,160,128]{2,1,0:T(8,128)}, u32[]{:S(2)}, u32[]{:S(2)}) collective-permute-start(f32[2,160,128]{2,1,0:T(8,128)} %get-tuple-element.21), channel_id=1, source_target_pairs={{1,0},{2,1},{3,2},{4,3},{5,4},{6,5},{7,6},{8,7},{9,8},{10,9},{11,1... | collective-permute-start | bytes 491528 | tf_op jit(solution)/shard_map/ppermute | solution.py:470
  25.6 1.1 %copy-start.1 = (f32[5,125,256]{2,1,0:T(8,128)S(1)}, f32[5,125,256]{2,1,0:T(8,128)}, u32[]{:S(2)}) copy-start(f32[5,125,256]{2,1,0:T(8,128)} %adjoint_ref.1) | copy-start | bytes 1920004
  26.7 1.0 %copy-start.2 = (f32[3,216,125]{2,1,0:T(8,128)S(1)}, f32[3,216,125]{2,1,0:T(8,128)}, u32[]{:S(2)}) copy-start(f32[3,216,125]{2,1,0:T(8,128)} %enrich_ref.1) | copy-start | bytes 972004
  27.7 0.9 %copy-start.6 = (bf16[216,192]{1,0:T(8,128)(2,1)S(1)}, bf16[216,192]{1,0:T(8,128)(2,1)}, u32[]{:S(2)}) copy-start(bf16[216,192]{1,0:T(8,128)(2,1)} %constant.13.clone.lift_ref) | copy-start | bytes 248836
  28.6 0.8 %copy-start.7 = (f32[5,5,256]{2,1,0:T(8,128)S(1)}, f32[5,5,256]{2,1,0:T(8,128)}, u32[]{:S(2)}) copy-start(f32[5,5,256]{2,1,0:T(8,128)} %jacobian_ref.1) | copy-start | bytes 76804
  29.4 0.8 %copy-start.8 = (bf16[64,216]{1,0:T(8,128)(2,1)S(1)}, bf16[64,216]{1,0:T(8,128)(2,1)}, u32[]{:S(2)}) copy-start(bf16[64,216]{1,0:T(8,128)(2,1)} %constant.14.clone.lift_edge_ref) | copy-start | bytes 82948
  30.1 0.7 %copy-start.10 = (s32[6,256]{1,0:T(8,128)S(1)}, s32[6,256]{1,0:T(8,128)}, u32[]{:S(2)}) copy-start(s32[6,256]{1,0:T(8,128)} %near_ref.1) | copy-start | bytes 18436

commit v4 on v3

--- a/solution.py
+++ b/solution.py
@@ -14,6 +14,7 @@
 ND = 128
 HALF = 128
 QP = 32
+LOADS = ((0, 2), (2, 3))
 VMEM = 48 * 1024 * 1024
 
 
@@ -100,10 +101,14 @@
         pltpu.make_async_copy(order_hbm, order_ref, in_sems.at[0]),
         pltpu.make_async_copy(owner_hbm, owner_ref, in_sems.at[1]),
     ]
-    fields = [
-        pltpu.make_async_copy(state_hbm, state_ref, in_sems.at[2]),
-        pltpu.make_async_copy(adjoint_hbm, adjoint_ref, in_sems.at[3]),
-    ]
+    fields = []
+    for first, count in LOADS:
+        part = pl.ds(first, count)
+        k = len(fields) + 2
+        fields.append(pltpu.make_async_copy(state_hbm.at[part], state_ref.at[part], in_sems.at[k]))
+        fields.append(
+            pltpu.make_async_copy(adjoint_hbm.at[part], adjoint_ref.at[part], in_sems.at[k + 1])
+        )
     for copy in small:
         copy.start()
     for copy in fields:
@@ -151,10 +156,11 @@
         copy.start()
         sends.append(copy)
 
-    for copy in fields:
-        copy.wait()
-    for t in range(FIELDS):
-        send(t, gather(prepare(t)))
+    for g, (first, count) in enumerate(LOADS):
+        fields[2 * g].wait()
+        fields[2 * g + 1].wait()
+        for t in range(first, first + count):
+            send(t, gather(prepare(t)))
     for copy in sends:
         copy.wait()
 
@@ -173,7 +179,7 @@
             pltpu.VMEM((FIELDS, MODES, KE), jnp.float32),
             pltpu.VMEM((FIELDS, 256, KE), jnp.float32),
             pltpu.VMEM((FIELDS, ND // 2, 2, 8, 128), jnp.float32),
-            pltpu.SemaphoreType.DMA((4,)),
+            pltpu.SemaphoreType.DMA((2 + 2 * len(LOADS),)),
             pltpu.SemaphoreType.DMA((FIELDS,)),
         ],
         compiler_params=pltpu.CompilerParams(vmem_limit_bytes=VMEM),
@@ -337,11 +343,12 @@
     ids_ref,
     orders_ref,
     indicator_ref,
+    old_ref,
     in_sems,
     out_sems,
 ):
     loads = [
-        pltpu.make_async_copy(rows_hbm, rows_ref.at[pl.ds(0, 2 * RICH)], in_sems.at[0]),
+        pltpu.make_async_copy(rows_hbm, rows_ref, in_sems.at[0]),
         pltpu.make_async_copy(own_hbm, own_ref, in_sems.at[1]),
         pltpu.make_async_copy(edge_hbm, edge_ref, in_sems.at[2]),
         pltpu.make_async_copy(picks_hbm, picks_ref, in_sems.at[3]),
@@ -351,30 +358,20 @@
     for copy in loads:
         copy.start()
     slots = ND * CAP
-    n = lax.broadcasted_iota(jnp.int32, (RICH, 256), 0)
+    n = lax.broadcasted_iota(jnp.int32, (RICH, 128), 0)
     i = (n * 57) >> 11
     rest = n - i * 36
     j = (rest * 43) >> 8
-    k = rest - j * 6
-    top = jnp.maximum(jnp.maximum(i, j), k)
-    m = lax.broadcasted_iota(jnp.int32, (RICH, 256), 1) & 127
-    embed = jnp.where((top < 5) & (m == i * 25 + j * 5 + k), 1.0, 0.0).astype(jnp.bfloat16)
-    rows_ref[2 * RICH :, :] = embed
-    m = lax.broadcasted_iota(jnp.int32, (128, 256), 1) & 127
-    eye = jnp.where(m == lax.broadcasted_iota(jnp.int32, (128, 256), 0), 1.0, 0.0)
-    eye = eye.astype(jnp.bfloat16)
-    top = jnp.concatenate([top, top], axis=1)
+    top = jnp.maximum(jnp.maximum(i, j), rest - j * 6)
+    top = jnp.concatenate([top] * CAP, axis=1)
     upper = lax.broadcasted_iota(jnp.int32, (ND // 2, 8, 128), 1) >= CAP
+    old_ref[...] = jnp.zeros(old_ref.shape, jnp.float32)
     stores = []
 
     def store(source, target):
         copy = pltpu.make_async_copy(source, target, out_sems.at[len(stores)])
         copy.start()
         stores.append(copy)
-
-    def doubled(x):
-        high, low = parts(x.reshape(slots, 128))
-        return jnp.concatenate([high, low], axis=1)
 
     def finish():
         for copy in loads[1:]:
@@ -397,10 +394,6 @@
         state_ref[t] = moved[0:MODES, :]
         return moved
 
-    def put_adjoint(t, both, new_mask):
-        new = both[0:RICH] + both[RICH : 2 * RICH]
-        adjoint_ref[t] = both[2 * RICH :] + jnp.where(new_mask, new, 0.0)
-
     def labels(moved):
         id_row = moved[125:126, :].astype(jnp.int32)
         order_row = moved[126:127, :].astype(jnp.int32)
@@ -409,16 +402,19 @@
         orders_ref[...] = order_row
         return top == order_row + 1
 
-    moves = []
     for t in range(FIELDS):
-        state, adjoint = split(t)
-        moved = put_state(t, state)
+        moved = put_state(t, split(t)[0])
         if t == 0:
             new_mask = labels(moved)
     store(state_ref, state_hbm)
     loads[0].wait()
     for t in range(FIELDS):
-        put_adjoint(t, dot_nt(rows_ref[...], doubled(split(t)[1])), new_mask)
+        turned = split(t)[1].reshape(slots, 128).T
+        for g in range(25):
+            to = 36 * (g // 5) + 6 * (g % 5)
+            old_ref[t % 2, to : to + 5, :] = turned[5 * g : 5 * g + 5, :]
+        both = dot(rows_ref[...], jnp.concatenate(parts(turned), axis=0))
+        adjoint_ref[t] = jnp.where(new_mask, both[0:RICH] + both[RICH:], old_ref[t % 2])
         if t == 2:
             finish()
             store(indicator_ref, indicator_hbm)
@@ -445,13 +441,14 @@
         out_specs=(far,) * 5,
         out_shape=tuple(pltpu.HBM(*a) for a in shapes),
         scratch_shapes=[
-            pltpu.VMEM((3 * RICH, 256), jnp.bfloat16),
+            pltpu.VMEM((2 * RICH, 256), jnp.bfloat16),
             pltpu.VMEM((1, KE), jnp.float32),
             pltpu.VMEM((2, FIELDS * QP, KE), jnp.float32),
             pltpu.VMEM((2, KE, KE), jnp.bfloat16),
             pltpu.VMEM((2, 2, FIELDS * QP, HALF), jnp.float32),
         ]
         + [pltpu.VMEM(*a) for a in shapes]
+        + [pltpu.VMEM((2, RICH, slots), jnp.float32)]
         + [pltpu.SemaphoreType.DMA((6,)), pltpu.SemaphoreType.DMA((2 * FIELDS + 3,))],
         compiler_params=pltpu.CompilerParams(vmem_limit_bytes=VMEM),
         name="unpack",

time: 55.7 us -> 55.5 us (level)
  no operation moved by 1% of the time
where the time goes in v4:
time: 55.5 us; the launch traced here: 54.8 us
  starting transfers between devices  20.3 us (37%)
  waiting for transfers between devices  17.1 us (31%)
  Pallas kernels  11.4 us (21%)
  local copies, waits for them, and re-layouts  5.22 us (9%)
  between operations  0.76 us (1%)
    ppermute x1, waiting for transfers between devices, body(): before = lax.ppermute(last, 'dom', up)  17.1 us
    all_to_all x1, starting transfers between devices, body(): lax.all_to_all(message, 'dom', split_axis=0, concat_axis=0, tiled=True)  10.5 us
    ppermute x1, starting transfers between devices, body(): after = lax.ppermute(first, 'dom', down)  7.72 us
    unnamed x22, local copies, waits for them, and re-layouts  5.22 us
    pallas_call x1, Pallas kernels, own_indicators(): pl.pallas_call(indicator_kernel, in_specs=[pl.BlockSpec(memory_space=pltp...  3.75 us
    pallas_call x1, Pallas kernels, pack(): pl.pallas_call(pack_kernel, in_specs=[far] * 4, out_specs=far, out_shape=...  3.45 us
    pallas_call x1, Pallas kernels, unpack(): pl.pallas_call(unpack_kernel, in_specs=[pl.BlockSpec(memory_space=pltpu.V...  3.15 us
    ppermute x1, starting transfers between devices, body(): before = lax.ppermute(last, 'dom', up)  2.05 us
  transfers between devices with their start and end apart: 3, of which 1 were waited for; matrix products, arithmetic and copies ran while one was open for 0% of the time, Pallas kernels for 9%

profile of v4, /device:TPU:2, one launch (start us, length us, event | category | flops | bytes accessed | tf_op | source)
XLA Modules:
  0.0 54.8 jit_solution(6916472645200123031)
XLA Ops:
  0.6 3.4 %pack.1 = f32[64,2,40,128]{3,2,1,0:T(8,128)} custom-call(s32[1,256]{1,0:T(1,128)} %bitcast.7, s32[1,256]{1,0:T(1,128)} %bitcast.11, f32[5,125,256]{2,1,0:T(8,128)} %state_ref.3, f32[5,125,256]{2,1,0:T(8,128)} %adjoint_ref.1), custom_call_target="tpu_custom_call" | custom-call | tf_op jit(solution)/shard_map/pack/pallas_call | solution.py:170
  4.1 0.0 copy-start
  4.1 0.0 copy-start.3
  4.1 0.0 copy-start.9
  4.1 0.0 copy-start.4
  4.1 0.0 copy-start.5
  4.1 10.5 %all-to-all-start = ((f32[128,40,128]{2,1,0:T(8,128)}), f32[128,40,128]{2,1,0:T(8,128)S(1)}, u32[]{:S(2)}, u32[]{:S(2)}) async-start(f32[128,40,128]{2,1,0:T(8,128)} %bitcast.10), calls=%async_computation | async-start | bytes 5242880 | tf_op jit(solution)/shard_map/all_to_all | solution.py:462
  14.7 0.0 copy-done
  14.7 0.0 copy-done.3
  14.7 1.1 %edges.1 = (f32[2,160,128]{2,1,0:T(8,128)}, f32[2,160,128]{2,1,0:T(8,128)}) custom-call(s32[1,256]{1,0:T(1,128)S(1)} %bitcast.8, f32[5,125,256]{2,1,0:T(8,128)S(1)} %copy-done, bf16[192,125]{1,0:T(8,128)(2,1)S(1)} %copy-done.3), custom_call_target="tpu_custom_call" | custom-call | tf_op jit(solution)/shard_map/edges/pallas_call | solution.py:202
  15.8 2.0 %collective-permute-start = (f32[2,160,128]{2,1,0:T(8,128)}, f32[2,160,128]{2,1,0:T(8,128)}, u32[]{:S(2)}, u32[]{:S(2)}) collective-permute-start(f32[2,160,128]{2,1,0:T(8,128)} %get-tuple-element.20), channel_id=1, source_target_pairs={{0,1},{1,2},{2,3},{3,4},{4,5},{5,6},{6,7},{7,8},{8,9},{9,10},{10,1... | collective-permute-start | bytes 491528 | tf_op jit(solution)/shard_map/ppermute | solution.py:466
  17.8 7.7 %collective-permute-start.1 = (f32[2,160,128]{2,1,0:T(8,128)}, f32[2,160,128]{2,1,0:T(8,128)}, u32[]{:S(2)}, u32[]{:S(2)}) collective-permute-start(f32[2,160,128]{2,1,0:T(8,128)} %get-tuple-element.21), channel_id=1, source_target_pairs={{1,0},{2,1},{3,2},{4,3},{5,4},{6,5},{7,6},{8,7},{9,8},{10,9},{11,1... | collective-permute-start | bytes 491528 | tf_op jit(solution)/shard_map/ppermute | solution.py:467
  25.6 0.0 copy-start.1
  25.6 1.1 %copy-done.1 = f32[5,125,256]{2,1,0:T(8,128)S(1)} copy-done((f32[5,125,256]{2,1,0:T(8,128)S(1)}, f32[5,125,256]{2,1,0:T(8,128)}, u32[]{:S(2)}) %copy-start.1) | copy-done | bytes 640024
  26.7 1.0 %copy-done.2 = f32[3,216,125]{2,1,0:T(8,128)S(1)} copy-done((f32[3,216,125]{2,1,0:T(8,128)S(1)}, f32[3,216,125]{2,1,0:T(8,128)}, u32[]{:S(2)}) %copy-start.2) | copy-done | bytes 324024
  27.7 0.9 %copy-done.6 = bf16[216,192]{1,0:T(8,128)(2,1)S(1)} copy-done((bf16[216,192]{1,0:T(8,128)(2,1)S(1)}, bf16[216,192]{1,0:T(8,128)(2,1)}, u32[]{:S(2)}) %copy-start.6) | copy-done | bytes 82968
  28.6 0.8 %copy-done.7 = f32[5,5,256]{2,1,0:T(8,128)S(1)} copy-done((f32[5,5,256]{2,1,0:T(8,128)S(1)}, f32[5,5,256]{2,1,0:T(8,128)}, u32[]{:S(2)}) %copy-start.7) | copy-done | bytes 25624
  29.3 0.8 %copy-done.8 = bf16[64,216]{1,0:T(8,128)(2,1)S(1)} copy-done((bf16[64,216]{1,0:T(8,128)(2,1)S(1)}, bf16[64,216]{1,0:T(8,128)(2,1)}, u32[]{:S(2)}) %copy-start.8) | copy-done | bytes 27672
  30.1 0.7 %copy-done.10 = s32[6,256]{1,0:T(8,128)S(1)} copy-done((s32[6,256]{1,0:T(8,128)S(1)}, s32[6,256]{1,0:T(8,128)}, u32[]{:S(2)}) %copy-start.10) | copy-done | bytes 6168
  30.8 3.8 %own_indicators.1 = (f32[1,256]{1,0:T(1,128)}, bf16[432,256]{1,0:T(8,128)(2,1)}, f32[2,160,256]{2,1,0:T(8,128)}, bf16[2,256,256]{2,1,0:T(8,128)(2,1)}) custom-call(s32[1]{0:T(128)} %bitcast.3.device_ref, s32[1,256]{1,0:T(1,128)S(1)} %bitcast.9, s32[6,256]{1,0:T(8,128)S(1)} %copy-done.10, f32[5,125,256]{2,1,0:T(8,128)S(1)} %copy-done, ...), custom_call_target="tpu_custom_call" | custom-call | tf_op jit(solution)/shard_map/own_indicators/pallas_call | solution.py:289
  34.5 17.1 %collective-permute-done.before_hbm = f32[2,160,128]{2,1,0:T(8,128)} collective-permute-done((f32[2,160,128]{2,1,0:T(8,128)}, f32[2,160,128]{2,1,0:T(8,128)}, u32[]{:S(2)}, u32[]{:S(2)}) %collective-permute-start) | collective-permute-done | bytes 163872 | tf_op jit(solution)/shard_map/ppermute | solution.py:466
  51.6 0.0 collective-permute-done.1.after_hbm
  51.6 0.0 all-to-all-done.in_ref
  51.6 3.1 %unpack.1 = (f32[5,125,512]{2,1,0:T(8,128)}, f32[5,216,512]{2,1,0:T(8,128)}, s32[1,512]{1,0:T(1,128)}, s32[1,512]{1,0:T(1,128)}, f32[1,256]{1,0:T(1,128)}) custom-call(f32[128,40,128]{2,1,0:T(8,128)S(1)} %all-to-all-done.in_ref, bf16[432,256]{1,0:T(8,128)(2,1)} %get-tuple-element.16.rows_hbm, f32[1,256]{1,0:T(1,128)} %get-tuple-element.17.own_hbm, ...), custom_call_target="tpu_custom_call" | custom-call | tf_op jit(solution)/shard_map/unpack/pallas_call | solution.py:438
  (8 shorter events, 0.0 us)
Async XLA Ops:
  4.1 10.6 %copy-start = (f32[5,125,256]{2,1,0:T(8,128)S(1)}, f32[5,125,256]{2,1,0:T(8,128)}, u32[]{:S(2)}) copy-start(f32[5,125,256]{2,1,0:T(8,128)} %state_ref.3) | copy-start | bytes 1920004
  4.1 10.6 %copy-start.3 = (bf16[192,125]{1,0:T(8,128)(2,1)S(1)}, bf16[192,125]{1,0:T(8,128)(2,1)}, u32[]{:S(2)}) copy-start(bf16[192,125]{1,0:T(8,128)(2,1)} %constant.12.clone.trace_ref) | copy-start | bytes 144004
  4.1 10.6 %copy-start.9 = (s32[256]{0:T(256)S(1)}, s32[256]{0:T(256)}, u32[]{:S(2)}) copy-start(s32[256]{0:T(256)} %param.15) | copy-start | bytes 3076
  4.1 21.4 %copy-start.4 = (f32[216,125]{1,0:T(8,128)S(1)}, f32[216,125]{1,0:T(8,128)}, u32[]{:S(2)}) copy-start(f32[216,125]{1,0:T(8,128)} %volume_ref.1) | copy-start | bytes 324004
  4.1 21.4 %copy-start.5 = (f32[216,1]{1,0:T(8,128)S(1)}, f32[216,1]{1,0:T(8,128)}, u32[]{:S(2)}) copy-start(f32[216,1]{1,0:T(8,128)} %constant.15.clone.top_ref) | copy-start | bytes 2596
  4.1 47.5 %all-to-all-start = ((f32[128,40,128]{2,1,0:T(8,128)}), f32[128,40,128]{2,1,0:T(8,128)S(1)}, u32[]{:S(2)}, u32[]{:S(2)}) async-start(f32[128,40,128]{2,1,0:T(8,128)} %bitcast.10), calls=%async_computation | async-start | bytes 5242880 | tf_op jit(solution)/shard_map/all_to_all | solution.py:462
  15.8 35.9 %collective-permute-start = (f32[2,160,128]{2,1,0:T(8,128)}, f32[2,160,128]{2,1,0:T(8,128)}, u32[]{:S(2)}, u32[]{:S(2)}) collective-permute-start(f32[2,160,128]{2,1,0:T(8,128)} %get-tuple-element.20), channel_id=1, source_target_pairs={{0,1},{1,2},{2,3},{3,4},{4,5},{5,6},{6,7},{7,8},{8,9},{9,10},{10,1... | collective-permute-start | bytes 491528 | tf_op jit(solution)/shard_map/ppermute | solution.py:466
  17.8 33.8 %collective-permute-start.1 = (f32[2,160,128]{2,1,0:T(8,128)}, f32[2,160,128]{2,1,0:T(8,128)}, u32[]{:S(2)}, u32[]{:S(2)}) collective-permute-start(f32[2,160,128]{2,1,0:T(8,128)} %get-tuple-element.21), channel_id=1, source_target_pairs={{1,0},{2,1},{3,2},{4,3},{5,4},{6,5},{7,6},{8,7},{9,8},{10,9},{11,1... | collective-permute-start | bytes 491528 | tf_op jit(solution)/shard_map/ppermute | solution.py:467
  25.6 1.1 %copy-start.1 = (f32[5,125,256]{2,1,0:T(8,128)S(1)}, f32[5,125,256]{2,1,0:T(8,128)}, u32[]{:S(2)}) copy-start(f32[5,125,256]{2,1,0:T(8,128)} %adjoint_ref.1) | copy-start | bytes 1920004
  26.7 1.0 %copy-start.2 = (f32[3,216,125]{2,1,0:T(8,128)S(1)}, f32[3,216,125]{2,1,0:T(8,128)}, u32[]{:S(2)}) copy-start(f32[3,216,125]{2,1,0:T(8,128)} %enrich_ref.1) | copy-start | bytes 972004
  27.7 0.9 %copy-start.6 = (bf16[216,192]{1,0:T(8,128)(2,1)S(1)}, bf16[216,192]{1,0:T(8,128)(2,1)}, u32[]{:S(2)}) copy-start(bf16[216,192]{1,0:T(8,128)(2,1)} %constant.13.clone.lift_ref) | copy-start | bytes 248836
  28.5 0.8 %copy-start.7 = (f32[5,5,256]{2,1,0:T(8,128)S(1)}, f32[5,5,256]{2,1,0:T(8,128)}, u32[]{:S(2)}) copy-start(f32[5,5,256]{2,1,0:T(8,128)} %jacobian_ref.1) | copy-start | bytes 76804
  29.3 0.8 %copy-start.8 = (bf16[64,216]{1,0:T(8,128)(2,1)S(1)}, bf16[64,216]{1,0:T(8,128)(2,1)}, u32[]{:S(2)}) copy-start(bf16[64,216]{1,0:T(8,128)(2,1)} %constant.14.clone.lift_edge_ref) | copy-start | bytes 82948
  30.1 0.7 %copy-start.10 = (s32[6,256]{1,0:T(8,128)S(1)}, s32[6,256]{1,0:T(8,128)}, u32[]{:S(2)}) copy-start(s32[6,256]{1,0:T(8,128)} %near_ref.1) | copy-start | bytes 18436

commit v5 on v4

--- a/solution.py
+++ b/solution.py
@@ -413,14 +413,17 @@
         for g in range(25):
             to = 36 * (g // 5) + 6 * (g % 5)
             old_ref[t % 2, to : to + 5, :] = turned[5 * g : 5 * g + 5, :]
-        both = dot(rows_ref[...], jnp.concatenate(parts(turned), axis=0))
-        adjoint_ref[t] = jnp.where(new_mask, both[0:RICH] + both[RICH:], old_ref[t % 2])
+        high, low = parts(turned)
+        new = dot(rows_ref[0:RICH, :], jnp.concatenate([high, low], axis=0)) + dot(
+            rows_ref[RICH:, 0:128], high
+        )
+        adjoint_ref[t] = jnp.where(new_mask, new, old_ref[t % 2])
+        store(adjoint_ref.at[t], adjoint_hbm.at[t])
         if t == 2:
-            finish()
-            store(indicator_ref, indicator_hbm)
             store(ids_ref, ids_hbm)
             store(orders_ref, orders_hbm)
-        store(adjoint_ref.at[t], adjoint_hbm.at[t])
+    finish()
+    store(indicator_ref, indicator_hbm)
     for copy in stores:
         copy.wait()
 

time: 55.5 us -> 55.2 us (level)
  no operation moved by 1% of the time
where the time goes in v5:
time: 55.2 us; the launch traced here: 54.5 us
  starting transfers between devices  20.3 us (37%)
  waiting for transfers between devices  17.1 us (31%)
  Pallas kernels  11.2 us (20%)
  local copies, waits for them, and re-layouts  5.22 us (9%)
  between operations  0.76 us (1%)
    ppermute x1, waiting for transfers between devices, body(): before = lax.ppermute(last, 'dom', up)  17.1 us
    all_to_all x1, starting transfers between devices, body(): lax.all_to_all(message, 'dom', split_axis=0, concat_axis=0, tiled=True)  10.5 us
    ppermute x1, starting transfers between devices, body(): after = lax.ppermute(first, 'dom', down)  7.72 us
    unnamed x22, local copies, waits for them, and re-layouts  5.22 us
    pallas_call x1, Pallas kernels, own_indicators(): pl.pallas_call(indicator_kernel, in_specs=[pl.BlockSpec(memory_space=pltp...  3.75 us
    pallas_call x1, Pallas kernels, pack(): pl.pallas_call(pack_kernel, in_specs=[far] * 4, out_specs=far, out_shape=...  3.45 us
    pallas_call x1, Pallas kernels, unpack(): pl.pallas_call(unpack_kernel, in_specs=[pl.BlockSpec(memory_space=pltpu.V...  2.91 us
    ppermute x1, starting transfers between devices, body(): before = lax.ppermute(last, 'dom', up)  2.05 us
  transfers between devices with their start and end apart: 3, of which 1 were waited for; matrix products, arithmetic and copies ran while one was open for 0% of the time, Pallas kernels for 9%

profile of v5, /device:TPU:2, one launch (start us, length us, event | category | flops | bytes accessed | tf_op | source)
XLA Modules:
  0.0 54.5 jit_solution(4056143386534255212)
XLA Ops:
  0.6 3.4 %pack.1 = f32[64,2,40,128]{3,2,1,0:T(8,128)} custom-call(s32[1,256]{1,0:T(1,128)} %bitcast.7, s32[1,256]{1,0:T(1,128)} %bitcast.11, f32[5,125,256]{2,1,0:T(8,128)} %state_ref.3, f32[5,125,256]{2,1,0:T(8,128)} %adjoint_ref.1), custom_call_target="tpu_custom_call" | custom-call | tf_op jit(solution)/shard_map/pack/pallas_call | solution.py:170
  4.1 0.0 copy-start
  4.1 0.0 copy-start.3
  4.1 0.0 copy-start.9
  4.1 0.0 copy-start.4
  4.1 0.0 copy-start.5
  4.1 10.5 %all-to-all-start = ((f32[128,40,128]{2,1,0:T(8,128)}), f32[128,40,128]{2,1,0:T(8,128)S(1)}, u32[]{:S(2)}, u32[]{:S(2)}) async-start(f32[128,40,128]{2,1,0:T(8,128)} %bitcast.10), calls=%async_computation | async-start | bytes 5242880 | tf_op jit(solution)/shard_map/all_to_all | solution.py:465
  14.7 1.1 %edges.1 = (f32[2,160,128]{2,1,0:T(8,128)}, f32[2,160,128]{2,1,0:T(8,128)}) custom-call(s32[1,256]{1,0:T(1,128)S(1)} %bitcast.8, f32[5,125,256]{2,1,0:T(8,128)S(1)} %copy-done, bf16[192,125]{1,0:T(8,128)(2,1)S(1)} %copy-done.3), custom_call_target="tpu_custom_call" | custom-call | tf_op jit(solution)/shard_map/edges/pallas_call | solution.py:202
  15.8 2.0 %collective-permute-start = (f32[2,160,128]{2,1,0:T(8,128)}, f32[2,160,128]{2,1,0:T(8,128)}, u32[]{:S(2)}, u32[]{:S(2)}) collective-permute-start(f32[2,160,128]{2,1,0:T(8,128)} %get-tuple-element.20), channel_id=1, source_target_pairs={{0,1},{1,2},{2,3},{3,4},{4,5},{5,6},{6,7},{7,8},{8,9},{9,10},{10,1... | collective-permute-start | bytes 491528 | tf_op jit(solution)/shard_map/ppermute | solution.py:469
  17.8 7.7 %collective-permute-start.1 = (f32[2,160,128]{2,1,0:T(8,128)}, f32[2,160,128]{2,1,0:T(8,128)}, u32[]{:S(2)}, u32[]{:S(2)}) collective-permute-start(f32[2,160,128]{2,1,0:T(8,128)} %get-tuple-element.21), channel_id=1, source_target_pairs={{1,0},{2,1},{3,2},{4,3},{5,4},{6,5},{7,6},{8,7},{9,8},{10,9},{11,1... | collective-permute-start | bytes 491528 | tf_op jit(solution)/shard_map/ppermute | solution.py:470
  25.6 0.0 copy-done.4
  25.6 0.0 copy-done.5
  25.6 0.0 copy-start.1
  25.6 1.1 %copy-done.1 = f32[5,125,256]{2,1,0:T(8,128)S(1)} copy-done((f32[5,125,256]{2,1,0:T(8,128)S(1)}, f32[5,125,256]{2,1,0:T(8,128)}, u32[]{:S(2)}) %copy-start.1) | copy-done | bytes 640024
  26.7 1.0 %copy-done.2 = f32[3,216,125]{2,1,0:T(8,128)S(1)} copy-done((f32[3,216,125]{2,1,0:T(8,128)S(1)}, f32[3,216,125]{2,1,0:T(8,128)}, u32[]{:S(2)}) %copy-start.2) | copy-done | bytes 324024
  27.7 0.9 %copy-done.6 = bf16[216,192]{1,0:T(8,128)(2,1)S(1)} copy-done((bf16[216,192]{1,0:T(8,128)(2,1)S(1)}, bf16[216,192]{1,0:T(8,128)(2,1)}, u32[]{:S(2)}) %copy-start.6) | copy-done | bytes 82968
  28.6 0.8 %copy-done.7 = f32[5,5,256]{2,1,0:T(8,128)S(1)} copy-done((f32[5,5,256]{2,1,0:T(8,128)S(1)}, f32[5,5,256]{2,1,0:T(8,128)}, u32[]{:S(2)}) %copy-start.7) | copy-done | bytes 25624
  29.3 0.8 %copy-done.8 = bf16[64,216]{1,0:T(8,128)(2,1)S(1)} copy-done((bf16[64,216]{1,0:T(8,128)(2,1)S(1)}, bf16[64,216]{1,0:T(8,128)(2,1)}, u32[]{:S(2)}) %copy-start.8) | copy-done | bytes 27672
  30.1 0.7 %copy-done.10 = s32[6,256]{1,0:T(8,128)S(1)} copy-done((s32[6,256]{1,0:T(8,128)S(1)}, s32[6,256]{1,0:T(8,128)}, u32[]{:S(2)}) %copy-start.10) | copy-done | bytes 6168
  30.8 3.8 %own_indicators.1 = (f32[1,256]{1,0:T(1,128)}, bf16[432,256]{1,0:T(8,128)(2,1)}, f32[2,160,256]{2,1,0:T(8,128)}, bf16[2,256,256]{2,1,0:T(8,128)(2,1)}) custom-call(s32[1]{0:T(128)} %bitcast.3.device_ref, s32[1,256]{1,0:T(1,128)S(1)} %bitcast.9, s32[6,256]{1,0:T(8,128)S(1)} %copy-done.10, f32[5,125,256]{2,1,0:T(8,128)S(1)} %copy-done, ...), custom_call_target="tpu_custom_call" | custom-call | tf_op jit(solution)/shard_map/own_indicators/pallas_call | solution.py:289
  34.5 17.1 %collective-permute-done.before_hbm = f32[2,160,128]{2,1,0:T(8,128)} collective-permute-done((f32[2,160,128]{2,1,0:T(8,128)}, f32[2,160,128]{2,1,0:T(8,128)}, u32[]{:S(2)}, u32[]{:S(2)}) %collective-permute-start) | collective-permute-done | bytes 163872 | tf_op jit(solution)/shard_map/ppermute | solution.py:469
  51.6 0.0 collective-permute-done.1.after_hbm
  51.6 0.0 all-to-all-done.in_ref
  51.6 2.9 %unpack.1 = (f32[5,125,512]{2,1,0:T(8,128)}, f32[5,216,512]{2,1,0:T(8,128)}, s32[1,512]{1,0:T(1,128)}, s32[1,512]{1,0:T(1,128)}, f32[1,256]{1,0:T(1,128)}) custom-call(f32[128,40,128]{2,1,0:T(8,128)S(1)} %all-to-all-done.in_ref, bf16[432,256]{1,0:T(8,128)(2,1)} %get-tuple-element.16.rows_hbm, f32[1,256]{1,0:T(1,128)} %get-tuple-element.17.own_hbm, ...), custom_call_target="tpu_custom_call" | custom-call | tf_op jit(solution)/shard_map/unpack/pallas_call | solution.py:441
  (8 shorter events, 0.0 us)
Async XLA Ops:
  4.1 10.6 %copy-start = (f32[5,125,256]{2,1,0:T(8,128)S(1)}, f32[5,125,256]{2,1,0:T(8,128)}, u32[]{:S(2)}) copy-start(f32[5,125,256]{2,1,0:T(8,128)} %state_ref.3) | copy-start | bytes 1920004
  4.1 10.6 %copy-start.3 = (bf16[192,125]{1,0:T(8,128)(2,1)S(1)}, bf16[192,125]{1,0:T(8,128)(2,1)}, u32[]{:S(2)}) copy-start(bf16[192,125]{1,0:T(8,128)(2,1)} %constant.12.clone.trace_ref) | copy-start | bytes 144004
  4.1 10.6 %copy-start.9 = (s32[256]{0:T(256)S(1)}, s32[256]{0:T(256)}, u32[]{:S(2)}) copy-start(s32[256]{0:T(256)} %param.15) | copy-start | bytes 3076
  4.1 21.4 %copy-start.4 = (f32[216,125]{1,0:T(8,128)S(1)}, f32[216,125]{1,0:T(8,128)}, u32[]{:S(2)}) copy-start(f32[216,125]{1,0:T(8,128)} %volume_ref.1) | copy-start | bytes 324004
  4.1 21.4 %copy-start.5 = (f32[216,1]{1,0:T(8,128)S(1)}, f32[216,1]{1,0:T(8,128)}, u32[]{:S(2)}) copy-start(f32[216,1]{1,0:T(8,128)} %constant.15.clone.top_ref) | copy-start | bytes 2596
  4.1 47.5 %all-to-all-start = ((f32[128,40,128]{2,1,0:T(8,128)}), f32[128,40,128]{2,1,0:T(8,128)S(1)}, u32[]{:S(2)}, u32[]{:S(2)}) async-start(f32[128,40,128]{2,1,0:T(8,128)} %bitcast.10), calls=%async_computation | async-start | bytes 5242880 | tf_op jit(solution)/shard_map/all_to_all | solution.py:465
  15.8 35.9 %collective-permute-start = (f32[2,160,128]{2,1,0:T(8,128)}, f32[2,160,128]{2,1,0:T(8,128)}, u32[]{:S(2)}, u32[]{:S(2)}) collective-permute-start(f32[2,160,128]{2,1,0:T(8,128)} %get-tuple-element.20), channel_id=1, source_target_pairs={{0,1},{1,2},{2,3},{3,4},{4,5},{5,6},{6,7},{7,8},{8,9},{9,10},{10,1... | collective-permute-start | bytes 491528 | tf_op jit(solution)/shard_map/ppermute | solution.py:469
  17.8 33.8 %collective-permute-start.1 = (f32[2,160,128]{2,1,0:T(8,128)}, f32[2,160,128]{2,1,0:T(8,128)}, u32[]{:S(2)}, u32[]{:S(2)}) collective-permute-start(f32[2,160,128]{2,1,0:T(8,128)} %get-tuple-element.21), channel_id=1, source_target_pairs={{1,0},{2,1},{3,2},{4,3},{5,4},{6,5},{7,6},{8,7},{9,8},{10,9},{11,1... | collective-permute-start | bytes 491528 | tf_op jit(solution)/shard_map/ppermute | solution.py:470
  25.6 1.1 %copy-start.1 = (f32[5,125,256]{2,1,0:T(8,128)S(1)}, f32[5,125,256]{2,1,0:T(8,128)}, u32[]{:S(2)}) copy-start(f32[5,125,256]{2,1,0:T(8,128)} %adjoint_ref.1) | copy-start | bytes 1920004
  26.7 1.0 %copy-start.2 = (f32[3,216,125]{2,1,0:T(8,128)S(1)}, f32[3,216,125]{2,1,0:T(8,128)}, u32[]{:S(2)}) copy-start(f32[3,216,125]{2,1,0:T(8,128)} %enrich_ref.1) | copy-start | bytes 972004
  27.7 0.9 %copy-start.6 = (bf16[216,192]{1,0:T(8,128)(2,1)S(1)}, bf16[216,192]{1,0:T(8,128)(2,1)}, u32[]{:S(2)}) copy-start(bf16[216,192]{1,0:T(8,128)(2,1)} %constant.13.clone.lift_ref) | copy-start | bytes 248836
  28.5 0.8 %copy-start.7 = (f32[5,5,256]{2,1,0:T(8,128)S(1)}, f32[5,5,256]{2,1,0:T(8,128)}, u32[]{:S(2)}) copy-start(f32[5,5,256]{2,1,0:T(8,128)} %jacobian_ref.1) | copy-start | bytes 76804
  29.3 0.8 %copy-start.8 = (bf16[64,216]{1,0:T(8,128)(2,1)S(1)}, bf16[64,216]{1,0:T(8,128)(2,1)}, u32[]{:S(2)}) copy-start(bf16[64,216]{1,0:T(8,128)(2,1)} %constant.14.clone.lift_edge_ref) | copy-start | bytes 82948
  30.1 0.7 %copy-start.10 = (s32[6,256]{1,0:T(8,128)S(1)}, s32[6,256]{1,0:T(8,128)}, u32[]{:S(2)}) copy-start(s32[6,256]{1,0:T(8,128)} %near_ref.1) | copy-start | bytes 18436

commit v6 on v5

--- a/solution.py
+++ b/solution.py
@@ -9,6 +9,7 @@
 FIELDS = 5
 MODES = 125
 RICH = 216
+PAD = 224
 KE = 256
 CAP = 4
 ND = 128
@@ -254,10 +255,12 @@
         jnp.where(top == 4.0, enrich_ref[1], jnp.where(top == 5.0, enrich_ref[2], 0.0)),
     )
     enrich_parts = parts(enrich)
+    padded = jnp.concatenate([enrich, jnp.zeros((PAD - RICH, MODES), jnp.float32)], axis=0)
+    high, low = parts(padded)
     rows_ref[...] = jnp.zeros(rows_ref.shape, jnp.bfloat16)
-    rows_ref[0:RICH, 0:MODES] = enrich_parts[0]
-    rows_ref[0:RICH, 128 : 128 + MODES] = enrich_parts[0]
-    rows_ref[RICH:, 0:MODES] = enrich_parts[1]
+    rows_ref[0:PAD, 0:MODES] = high
+    rows_ref[0:PAD, 128 : 128 + MODES] = high
+    rows_ref[PAD:, 0:MODES] = low
     volume_parts = parts(volume_ref[...])
     new_mask = top == order_row.astype(jnp.float32) + 1.0
     total = jnp.zeros((RICH, KE), jnp.float32)
@@ -292,7 +295,7 @@
         out_specs=(space,) * 4,
         out_shape=(
             pltpu.HBM((1, KE), jnp.float32),
-            pltpu.HBM((2 * RICH, 256), jnp.bfloat16),
+            pltpu.HBM((2 * PAD, 256), jnp.bfloat16),
             pltpu.HBM((2, FIELDS * QP, KE), jnp.float32),
             pltpu.HBM((2, KE, KE), jnp.bfloat16),
         ),
@@ -414,10 +417,10 @@
             to = 36 * (g // 5) + 6 * (g % 5)
             old_ref[t % 2, to : to + 5, :] = turned[5 * g : 5 * g + 5, :]
         high, low = parts(turned)
-        new = dot(rows_ref[0:RICH, :], jnp.concatenate([high, low], axis=0)) + dot(
-            rows_ref[RICH:, 0:128], high
+        new = dot(rows_ref[0:PAD, :], jnp.concatenate([high, low], axis=0)) + dot(
+            rows_ref[PAD:, 0:128], high
         )
-        adjoint_ref[t] = jnp.where(new_mask, new, old_ref[t % 2])
+        adjoint_ref[t] = jnp.where(new_mask, new[0:RICH], old_ref[t % 2])
         store(adjoint_ref.at[t], adjoint_hbm.at[t])
         if t == 2:
             store(ids_ref, ids_hbm)
@@ -444,7 +447,7 @@
         out_specs=(far,) * 5,
         out_shape=tuple(pltpu.HBM(*a) for a in shapes),
         scratch_shapes=[
-            pltpu.VMEM((2 * RICH, 256), jnp.bfloat16),
+            pltpu.VMEM((2 * PAD, 256), jnp.bfloat16),
             pltpu.VMEM((1, KE), jnp.float32),
             pltpu.VMEM((2, FIELDS * QP, KE), jnp.float32),
             pltpu.VMEM((2, KE, KE), jnp.bfloat16),

time: 55.2 us -> 55.2 us (level)
  no operation moved by 1% of the time
where the time goes in v6:
time: 55.2 us; the launch traced here: 54.6 us
  starting transfers between devices  20.3 us (37%)
  waiting for transfers between devices  17.1 us (31%)
  Pallas kernels  11.2 us (20%)
  local copies, waits for them, and re-layouts  5.22 us (9%)
  between operations  0.76 us (1%)
    ppermute x1, waiting for transfers between devices, body(): before = lax.ppermute(last, 'dom', up)  17.1 us
    all_to_all x1, starting transfers between devices, body(): lax.all_to_all(message, 'dom', split_axis=0, concat_axis=0, tiled=True)  10.5 us
    ppermute x1, starting transfers between devices, body(): after = lax.ppermute(first, 'dom', down)  7.72 us
    unnamed x22, local copies, waits for them, and re-layouts  5.22 us
    pallas_call x1, Pallas kernels, own_indicators(): pl.pallas_call(indicator_kernel, in_specs=[pl.BlockSpec(memory_space=pltp...  3.79 us
    pallas_call x1, Pallas kernels, pack(): pl.pallas_call(pack_kernel, in_specs=[far] * 4, out_specs=far, out_shape=...  3.45 us
    pallas_call x1, Pallas kernels, unpack(): pl.pallas_call(unpack_kernel, in_specs=[pl.BlockSpec(memory_space=pltpu.V...  2.92 us
    ppermute x1, starting transfers between devices, body(): before = lax.ppermute(last, 'dom', up)  2.05 us
  transfers between devices with their start and end apart: 3, of which 1 were waited for; matrix products, arithmetic and copies ran while one was open for 0% of the time, Pallas kernels for 9%

profile of v6, /device:TPU:2, one launch (start us, length us, event | category | flops | bytes accessed | tf_op | source)
XLA Modules:
  0.0 54.6 jit_solution(18009142232149431512)
XLA Ops:
  0.6 3.4 %pack.1 = f32[64,2,40,128]{3,2,1,0:T(8,128)} custom-call(s32[1,256]{1,0:T(1,128)} %bitcast.7, s32[1,256]{1,0:T(1,128)} %bitcast.11, f32[5,125,256]{2,1,0:T(8,128)} %state_ref.3, f32[5,125,256]{2,1,0:T(8,128)} %adjoint_ref.1), custom_call_target="tpu_custom_call" | custom-call | tf_op jit(solution)/shard_map/pack/pallas_call | solution.py:171
  4.1 0.0 copy-start
  4.1 0.0 copy-start.3
  4.1 0.0 copy-start.9
  4.1 0.0 copy-start.4
  4.1 0.0 copy-start.5
  4.1 10.5 %all-to-all-start = ((f32[128,40,128]{2,1,0:T(8,128)}), f32[128,40,128]{2,1,0:T(8,128)S(1)}, u32[]{:S(2)}, u32[]{:S(2)}) async-start(f32[128,40,128]{2,1,0:T(8,128)} %bitcast.10), calls=%async_computation | async-start | bytes 5242880 | tf_op jit(solution)/shard_map/all_to_all | solution.py:468
  14.7 0.0 copy-done
  14.7 0.0 copy-done.3
  14.7 1.1 %edges.1 = (f32[2,160,128]{2,1,0:T(8,128)}, f32[2,160,128]{2,1,0:T(8,128)}) custom-call(s32[1,256]{1,0:T(1,128)S(1)} %bitcast.8, f32[5,125,256]{2,1,0:T(8,128)S(1)} %copy-done, bf16[192,125]{1,0:T(8,128)(2,1)S(1)} %copy-done.3), custom_call_target="tpu_custom_call" | custom-call | tf_op jit(solution)/shard_map/edges/pallas_call | solution.py:203
  15.8 2.0 %collective-permute-start = (f32[2,160,128]{2,1,0:T(8,128)}, f32[2,160,128]{2,1,0:T(8,128)}, u32[]{:S(2)}, u32[]{:S(2)}) collective-permute-start(f32[2,160,128]{2,1,0:T(8,128)} %get-tuple-element.20), channel_id=1, source_target_pairs={{0,1},{1,2},{2,3},{3,4},{4,5},{5,6},{6,7},{7,8},{8,9},{9,10},{10,1... | collective-permute-start | bytes 491528 | tf_op jit(solution)/shard_map/ppermute | solution.py:472
  17.8 7.7 %collective-permute-start.1 = (f32[2,160,128]{2,1,0:T(8,128)}, f32[2,160,128]{2,1,0:T(8,128)}, u32[]{:S(2)}, u32[]{:S(2)}) collective-permute-start(f32[2,160,128]{2,1,0:T(8,128)} %get-tuple-element.21), channel_id=1, source_target_pairs={{1,0},{2,1},{3,2},{4,3},{5,4},{6,5},{7,6},{8,7},{9,8},{10,9},{11,1... | collective-permute-start | bytes 491528 | tf_op jit(solution)/shard_map/ppermute | solution.py:473
  25.6 0.0 copy-start.1
  25.6 1.1 %copy-done.1 = f32[5,125,256]{2,1,0:T(8,128)S(1)} copy-done((f32[5,125,256]{2,1,0:T(8,128)S(1)}, f32[5,125,256]{2,1,0:T(8,128)}, u32[]{:S(2)}) %copy-start.1) | copy-done | bytes 640024
  26.7 1.0 %copy-done.2 = f32[3,216,125]{2,1,0:T(8,128)S(1)} copy-done((f32[3,216,125]{2,1,0:T(8,128)S(1)}, f32[3,216,125]{2,1,0:T(8,128)}, u32[]{:S(2)}) %copy-start.2) | copy-done | bytes 324024
  27.7 0.9 %copy-done.6 = bf16[216,192]{1,0:T(8,128)(2,1)S(1)} copy-done((bf16[216,192]{1,0:T(8,128)(2,1)S(1)}, bf16[216,192]{1,0:T(8,128)(2,1)}, u32[]{:S(2)}) %copy-start.6) | copy-done | bytes 82968
  28.6 0.8 %copy-done.7 = f32[5,5,256]{2,1,0:T(8,128)S(1)} copy-done((f32[5,5,256]{2,1,0:T(8,128)S(1)}, f32[5,5,256]{2,1,0:T(8,128)}, u32[]{:S(2)}) %copy-start.7) | copy-done | bytes 25624
  29.3 0.8 %copy-done.8 = bf16[64,216]{1,0:T(8,128)(2,1)S(1)} copy-done((bf16[64,216]{1,0:T(8,128)(2,1)S(1)}, bf16[64,216]{1,0:T(8,128)(2,1)}, u32[]{:S(2)}) %copy-start.8) | copy-done | bytes 27672
  30.1 0.7 %copy-done.10 = s32[6,256]{1,0:T(8,128)S(1)} copy-done((s32[6,256]{1,0:T(8,128)S(1)}, s32[6,256]{1,0:T(8,128)}, u32[]{:S(2)}) %copy-start.10) | copy-done | bytes 6168
  30.8 3.8 %own_indicators.1 = (f32[1,256]{1,0:T(1,128)}, bf16[448,256]{1,0:T(8,128)(2,1)}, f32[2,160,256]{2,1,0:T(8,128)}, bf16[2,256,256]{2,1,0:T(8,128)(2,1)}) custom-call(s32[1]{0:T(128)} %bitcast.3.device_ref, s32[1,256]{1,0:T(1,128)S(1)} %bitcast.9, s32[6,256]{1,0:T(8,128)S(1)} %copy-done.10, f32[5,125,256]{2,1,0:T(8,128)S(1)} %copy-done, ...), custom_call_target="tpu_custom_call" | custom-call | tf_op jit(solution)/shard_map/own_indicators/pallas_call | solution.py:292
  34.6 17.1 %collective-permute-done.before_hbm = f32[2,160,128]{2,1,0:T(8,128)} collective-permute-done((f32[2,160,128]{2,1,0:T(8,128)}, f32[2,160,128]{2,1,0:T(8,128)}, u32[]{:S(2)}, u32[]{:S(2)}) %collective-permute-start) | collective-permute-done | bytes 163872 | tf_op jit(solution)/shard_map/ppermute | solution.py:472
  51.6 0.0 collective-permute-done.1.after_hbm
  51.6 0.0 all-to-all-done.in_ref
  51.6 2.9 %unpack.1 = (f32[5,125,512]{2,1,0:T(8,128)}, f32[5,216,512]{2,1,0:T(8,128)}, s32[1,512]{1,0:T(1,128)}, s32[1,512]{1,0:T(1,128)}, f32[1,256]{1,0:T(1,128)}) custom-call(f32[128,40,128]{2,1,0:T(8,128)S(1)} %all-to-all-done.in_ref, bf16[448,256]{1,0:T(8,128)(2,1)} %get-tuple-element.16.rows_hbm, f32[1,256]{1,0:T(1,128)} %get-tuple-element.17.own_hbm, ...), custom_call_target="tpu_custom_call" | custom-call | tf_op jit(solution)/shard_map/unpack/pallas_call | solution.py:444
  (8 shorter events, 0.0 us)
Async XLA Ops:
  4.1 10.6 %copy-start = (f32[5,125,256]{2,1,0:T(8,128)S(1)}, f32[5,125,256]{2,1,0:T(8,128)}, u32[]{:S(2)}) copy-start(f32[5,125,256]{2,1,0:T(8,128)} %state_ref.3) | copy-start | bytes 1920004
  4.1 10.6 %copy-start.3 = (bf16[192,125]{1,0:T(8,128)(2,1)S(1)}, bf16[192,125]{1,0:T(8,128)(2,1)}, u32[]{:S(2)}) copy-start(bf16[192,125]{1,0:T(8,128)(2,1)} %constant.12.clone.trace_ref) | copy-start | bytes 144004
  4.1 10.6 %copy-start.9 = (s32[256]{0:T(256)S(1)}, s32[256]{0:T(256)}, u32[]{:S(2)}) copy-start(s32[256]{0:T(256)} %param.15) | copy-start | bytes 3076
  4.1 21.4 %copy-start.4 = (f32[216,125]{1,0:T(8,128)S(1)}, f32[216,125]{1,0:T(8,128)}, u32[]{:S(2)}) copy-start(f32[216,125]{1,0:T(8,128)} %volume_ref.1) | copy-start | bytes 324004
  4.1 21.4 %copy-start.5 = (f32[216,1]{1,0:T(8,128)S(1)}, f32[216,1]{1,0:T(8,128)}, u32[]{:S(2)}) copy-start(f32[216,1]{1,0:T(8,128)} %constant.15.clone.top_ref) | copy-start | bytes 2596
  4.1 47.5 %all-to-all-start = ((f32[128,40,128]{2,1,0:T(8,128)}), f32[128,40,128]{2,1,0:T(8,128)S(1)}, u32[]{:S(2)}, u32[]{:S(2)}) async-start(f32[128,40,128]{2,1,0:T(8,128)} %bitcast.10), calls=%async_computation | async-start | bytes 5242880 | tf_op jit(solution)/shard_map/all_to_all | solution.py:468
  15.8 35.9 %collective-permute-start = (f32[2,160,128]{2,1,0:T(8,128)}, f32[2,160,128]{2,1,0:T(8,128)}, u32[]{:S(2)}, u32[]{:S(2)}) collective-permute-start(f32[2,160,128]{2,1,0:T(8,128)} %get-tuple-element.20), channel_id=1, source_target_pairs={{0,1},{1,2},{2,3},{3,4},{4,5},{5,6},{6,7},{7,8},{8,9},{9,10},{10,1... | collective-permute-start | bytes 491528 | tf_op jit(solution)/shard_map/ppermute | solution.py:472
  17.8 33.8 %collective-permute-start.1 = (f32[2,160,128]{2,1,0:T(8,128)}, f32[2,160,128]{2,1,0:T(8,128)}, u32[]{:S(2)}, u32[]{:S(2)}) collective-permute-start(f32[2,160,128]{2,1,0:T(8,128)} %get-tuple-element.21), channel_id=1, source_target_pairs={{1,0},{2,1},{3,2},{4,3},{5,4},{6,5},{7,6},{8,7},{9,8},{10,9},{11,1... | collective-permute-start | bytes 491528 | tf_op jit(solution)/shard_map/ppermute | solution.py:473
  25.6 1.1 %copy-start.1 = (f32[5,125,256]{2,1,0:T(8,128)S(1)}, f32[5,125,256]{2,1,0:T(8,128)}, u32[]{:S(2)}) copy-start(f32[5,125,256]{2,1,0:T(8,128)} %adjoint_ref.1) | copy-start | bytes 1920004
  26.7 1.0 %copy-start.2 = (f32[3,216,125]{2,1,0:T(8,128)S(1)}, f32[3,216,125]{2,1,0:T(8,128)}, u32[]{:S(2)}) copy-start(f32[3,216,125]{2,1,0:T(8,128)} %enrich_ref.1) | copy-start | bytes 972004
  27.7 0.9 %copy-start.6 = (bf16[216,192]{1,0:T(8,128)(2,1)S(1)}, bf16[216,192]{1,0:T(8,128)(2,1)}, u32[]{:S(2)}) copy-start(bf16[216,192]{1,0:T(8,128)(2,1)} %constant.13.clone.lift_ref) | copy-start | bytes 248836
  28.5 0.8 %copy-start.7 = (f32[5,5,256]{2,1,0:T(8,128)S(1)}, f32[5,5,256]{2,1,0:T(8,128)}, u32[]{:S(2)}) copy-start(f32[5,5,256]{2,1,0:T(8,128)} %jacobian_ref.1) | copy-start | bytes 76804
  29.3 0.8 %copy-start.8 = (bf16[64,216]{1,0:T(8,128)(2,1)S(1)}, bf16[64,216]{1,0:T(8,128)(2,1)}, u32[]{:S(2)}) copy-start(bf16[64,216]{1,0:T(8,128)(2,1)} %constant.14.clone.lift_edge_ref) | copy-start | bytes 82948
  30.1 0.7 %copy-start.10 = (s32[6,256]{1,0:T(8,128)S(1)}, s32[6,256]{1,0:T(8,128)}, u32[]{:S(2)}) copy-start(s32[6,256]{1,0:T(8,128)} %near_ref.1) | copy-start | bytes 18436

commit v7 on v6

--- a/solution.py
+++ b/solution.py
@@ -358,8 +358,7 @@
         pltpu.make_async_copy(before_hbm, halo_ref.at[0], in_sems.at[4]),
         pltpu.make_async_copy(after_hbm, halo_ref.at[1], in_sems.at[5]),
     ]
-    for copy in loads:
-        copy.start()
+    loads[0].start()
     slots = ND * CAP
     n = lax.broadcasted_iota(jnp.int32, (RICH, 128), 0)
     i = (n * 57) >> 11
@@ -410,6 +409,8 @@
         if t == 0:
             new_mask = labels(moved)
     store(state_ref, state_hbm)
+    for copy in loads[1:]:
+        copy.start()
     loads[0].wait()
     for t in range(FIELDS):
         turned = split(t)[1].reshape(slots, 128).T

time: 55.2 us -> 55.2 us (level)
  no operation moved by 1% of the time
where the time goes in v7:
time: 55.2 us; the launch traced here: 54.6 us
  starting transfers between devices  20.3 us (37%)
  waiting for transfers between devices  17.1 us (31%)
  Pallas kernels  11.2 us (20%)
  local copies, waits for them, and re-layouts  5.22 us (9%)
  between operations  0.76 us (1%)
    ppermute x1, waiting for transfers between devices, body(): before = lax.ppermute(last, 'dom', up)  17.1 us
    all_to_all x1, starting transfers between devices, body(): lax.all_to_all(message, 'dom', split_axis=0, concat_axis=0, tiled=True)  10.5 us
    ppermute x1, starting transfers between devices, body(): after = lax.ppermute(first, 'dom', down)  7.72 us
    unnamed x22, local copies, waits for them, and re-layouts  5.22 us
    pallas_call x1, Pallas kernels, own_indicators(): pl.pallas_call(indicator_kernel, in_specs=[pl.BlockSpec(memory_space=pltp...  3.79 us
    pallas_call x1, Pallas kernels, pack(): pl.pallas_call(pack_kernel, in_specs=[far] * 4, out_specs=far, out_shape=...  3.45 us
    pallas_call x1, Pallas kernels, unpack(): pl.pallas_call(unpack_kernel, in_specs=[pl.BlockSpec(memory_space=pltpu.V...  2.92 us
    ppermute x1, starting transfers between devices, body(): before = lax.ppermute(last, 'dom', up)  2.05 us
  transfers between devices with their start and end apart: 3, of which 1 were waited for; matrix products, arithmetic and copies ran while one was open for 0% of the time, Pallas kernels for 9%

profile of v7, /device:TPU:2, one launch (start us, length us, event | category | flops | bytes accessed | tf_op | source)
XLA Modules:
  0.0 54.6 jit_solution(2793615735941581120)
XLA Ops:
  0.6 3.4 %pack.1 = f32[64,2,40,128]{3,2,1,0:T(8,128)} custom-call(s32[1,256]{1,0:T(1,128)} %bitcast.7, s32[1,256]{1,0:T(1,128)} %bitcast.11, f32[5,125,256]{2,1,0:T(8,128)} %state_ref.3, f32[5,125,256]{2,1,0:T(8,128)} %adjoint_ref.1), custom_call_target="tpu_custom_call" | custom-call | tf_op jit(solution)/shard_map/pack/pallas_call | solution.py:171
  4.1 0.0 copy-start
  4.1 0.0 copy-start.3
  4.1 0.0 copy-start.9
  4.1 0.0 copy-start.4
  4.1 0.0 copy-start.5
  4.1 10.5 %all-to-all-start = ((f32[128,40,128]{2,1,0:T(8,128)}), f32[128,40,128]{2,1,0:T(8,128)S(1)}, u32[]{:S(2)}, u32[]{:S(2)}) async-start(f32[128,40,128]{2,1,0:T(8,128)} %bitcast.10), calls=%async_computation | async-start | bytes 5242880 | tf_op jit(solution)/shard_map/all_to_all | solution.py:469
  14.7 0.0 copy-done
  14.7 0.0 copy-done.3
  14.7 1.1 %edges.1 = (f32[2,160,128]{2,1,0:T(8,128)}, f32[2,160,128]{2,1,0:T(8,128)}) custom-call(s32[1,256]{1,0:T(1,128)S(1)} %bitcast.8, f32[5,125,256]{2,1,0:T(8,128)S(1)} %copy-done, bf16[192,125]{1,0:T(8,128)(2,1)S(1)} %copy-done.3), custom_call_target="tpu_custom_call" | custom-call | tf_op jit(solution)/shard_map/edges/pallas_call | solution.py:203
  15.8 2.0 %collective-permute-start = (f32[2,160,128]{2,1,0:T(8,128)}, f32[2,160,128]{2,1,0:T(8,128)}, u32[]{:S(2)}, u32[]{:S(2)}) collective-permute-start(f32[2,160,128]{2,1,0:T(8,128)} %get-tuple-element.20), channel_id=1, source_target_pairs={{0,1},{1,2},{2,3},{3,4},{4,5},{5,6},{6,7},{7,8},{8,9},{9,10},{10,1... | collective-permute-start | bytes 491528 | tf_op jit(solution)/shard_map/ppermute | solution.py:473
  17.8 7.7 %collective-permute-start.1 = (f32[2,160,128]{2,1,0:T(8,128)}, f32[2,160,128]{2,1,0:T(8,128)}, u32[]{:S(2)}, u32[]{:S(2)}) collective-permute-start(f32[2,160,128]{2,1,0:T(8,128)} %get-tuple-element.21), channel_id=1, source_target_pairs={{1,0},{2,1},{3,2},{4,3},{5,4},{6,5},{7,6},{8,7},{9,8},{10,9},{11,1... | collective-permute-start | bytes 491528 | tf_op jit(solution)/shard_map/ppermute | solution.py:474
  25.6 0.0 copy-start.1
  25.6 1.1 %copy-done.1 = f32[5,125,256]{2,1,0:T(8,128)S(1)} copy-done((f32[5,125,256]{2,1,0:T(8,128)S(1)}, f32[5,125,256]{2,1,0:T(8,128)}, u32[]{:S(2)}) %copy-start.1) | copy-done | bytes 640024
  26.7 1.0 %copy-done.2 = f32[3,216,125]{2,1,0:T(8,128)S(1)} copy-done((f32[3,216,125]{2,1,0:T(8,128)S(1)}, f32[3,216,125]{2,1,0:T(8,128)}, u32[]{:S(2)}) %copy-start.2) | copy-done | bytes 324024
  27.7 0.9 %copy-done.6 = bf16[216,192]{1,0:T(8,128)(2,1)S(1)} copy-done((bf16[216,192]{1,0:T(8,128)(2,1)S(1)}, bf16[216,192]{1,0:T(8,128)(2,1)}, u32[]{:S(2)}) %copy-start.6) | copy-done | bytes 82968
  28.6 0.8 %copy-done.7 = f32[5,5,256]{2,1,0:T(8,128)S(1)} copy-done((f32[5,5,256]{2,1,0:T(8,128)S(1)}, f32[5,5,256]{2,1,0:T(8,128)}, u32[]{:S(2)}) %copy-start.7) | copy-done | bytes 25624
  29.3 0.8 %copy-done.8 = bf16[64,216]{1,0:T(8,128)(2,1)S(1)} copy-done((bf16[64,216]{1,0:T(8,128)(2,1)S(1)}, bf16[64,216]{1,0:T(8,128)(2,1)}, u32[]{:S(2)}) %copy-start.8) | copy-done | bytes 27672
  30.1 0.7 %copy-done.10 = s32[6,256]{1,0:T(8,128)S(1)} copy-done((s32[6,256]{1,0:T(8,128)S(1)}, s32[6,256]{1,0:T(8,128)}, u32[]{:S(2)}) %copy-start.10) | copy-done | bytes 6168
  30.8 3.8 %own_indicators.1 = (f32[1,256]{1,0:T(1,128)}, bf16[448,256]{1,0:T(8,128)(2,1)}, f32[2,160,256]{2,1,0:T(8,128)}, bf16[2,256,256]{2,1,0:T(8,128)(2,1)}) custom-call(s32[1]{0:T(128)} %bitcast.3.device_ref, s32[1,256]{1,0:T(1,128)S(1)} %bitcast.9, s32[6,256]{1,0:T(8,128)S(1)} %copy-done.10, f32[5,125,256]{2,1,0:T(8,128)S(1)} %copy-done, ...), custom_call_target="tpu_custom_call" | custom-call | tf_op jit(solution)/shard_map/own_indicators/pallas_call | solution.py:292
  34.6 17.1 %collective-permute-done.before_hbm = f32[2,160,128]{2,1,0:T(8,128)} collective-permute-done((f32[2,160,128]{2,1,0:T(8,128)}, f32[2,160,128]{2,1,0:T(8,128)}, u32[]{:S(2)}, u32[]{:S(2)}) %collective-permute-start) | collective-permute-done | bytes 163872 | tf_op jit(solution)/shard_map/ppermute | solution.py:473
  51.6 0.0 collective-permute-done.1.after_hbm
  51.6 0.0 all-to-all-done.in_ref
  51.6 2.9 %unpack.1 = (f32[5,125,512]{2,1,0:T(8,128)}, f32[5,216,512]{2,1,0:T(8,128)}, s32[1,512]{1,0:T(1,128)}, s32[1,512]{1,0:T(1,128)}, f32[1,256]{1,0:T(1,128)}) custom-call(f32[128,40,128]{2,1,0:T(8,128)S(1)} %all-to-all-done.in_ref, bf16[448,256]{1,0:T(8,128)(2,1)} %get-tuple-element.16.rows_hbm, f32[1,256]{1,0:T(1,128)} %get-tuple-element.17.own_hbm, ...), custom_call_target="tpu_custom_call" | custom-call | tf_op jit(solution)/shard_map/unpack/pallas_call | solution.py:445
  (8 shorter events, 0.0 us)
Async XLA Ops:
  4.1 10.6 %copy-start = (f32[5,125,256]{2,1,0:T(8,128)S(1)}, f32[5,125,256]{2,1,0:T(8,128)}, u32[]{:S(2)}) copy-start(f32[5,125,256]{2,1,0:T(8,128)} %state_ref.3) | copy-start | bytes 1920004
  4.1 10.6 %copy-start.3 = (bf16[192,125]{1,0:T(8,128)(2,1)S(1)}, bf16[192,125]{1,0:T(8,128)(2,1)}, u32[]{:S(2)}) copy-start(bf16[192,125]{1,0:T(8,128)(2,1)} %constant.12.clone.trace_ref) | copy-start | bytes 144004
  4.1 10.6 %copy-start.9 = (s32[256]{0:T(256)S(1)}, s32[256]{0:T(256)}, u32[]{:S(2)}) copy-start(s32[256]{0:T(256)} %param.15) | copy-start | bytes 3076
  4.1 21.4 %copy-start.4 = (f32[216,125]{1,0:T(8,128)S(1)}, f32[216,125]{1,0:T(8,128)}, u32[]{:S(2)}) copy-start(f32[216,125]{1,0:T(8,128)} %volume_ref.1) | copy-start | bytes 324004
  4.1 21.4 %copy-start.5 = (f32[216,1]{1,0:T(8,128)S(1)}, f32[216,1]{1,0:T(8,128)}, u32[]{:S(2)}) copy-start(f32[216,1]{1,0:T(8,128)} %constant.15.clone.top_ref) | copy-start | bytes 2596
  4.1 47.5 %all-to-all-start = ((f32[128,40,128]{2,1,0:T(8,128)}), f32[128,40,128]{2,1,0:T(8,128)S(1)}, u32[]{:S(2)}, u32[]{:S(2)}) async-start(f32[128,40,128]{2,1,0:T(8,128)} %bitcast.10), calls=%async_computation | async-start | bytes 5242880 | tf_op jit(solution)/shard_map/all_to_all | solution.py:469
  15.8 35.9 %collective-permute-start = (f32[2,160,128]{2,1,0:T(8,128)}, f32[2,160,128]{2,1,0:T(8,128)}, u32[]{:S(2)}, u32[]{:S(2)}) collective-permute-start(f32[2,160,128]{2,1,0:T(8,128)} %get-tuple-element.20), channel_id=1, source_target_pairs={{0,1},{1,2},{2,3},{3,4},{4,5},{5,6},{6,7},{7,8},{8,9},{9,10},{10,1... | collective-permute-start | bytes 491528 | tf_op jit(solution)/shard_map/ppermute | solution.py:473
  17.8 33.8 %collective-permute-start.1 = (f32[2,160,128]{2,1,0:T(8,128)}, f32[2,160,128]{2,1,0:T(8,128)}, u32[]{:S(2)}, u32[]{:S(2)}) collective-permute-start(f32[2,160,128]{2,1,0:T(8,128)} %get-tuple-element.21), channel_id=1, source_target_pairs={{1,0},{2,1},{3,2},{4,3},{5,4},{6,5},{7,6},{8,7},{9,8},{10,9},{11,1... | collective-permute-start | bytes 491528 | tf_op jit(solution)/shard_map/ppermute | solution.py:474
  25.6 1.1 %copy-start.1 = (f32[5,125,256]{2,1,0:T(8,128)S(1)}, f32[5,125,256]{2,1,0:T(8,128)}, u32[]{:S(2)}) copy-start(f32[5,125,256]{2,1,0:T(8,128)} %adjoint_ref.1) | copy-start | bytes 1920004
  26.7 1.0 %copy-start.2 = (f32[3,216,125]{2,1,0:T(8,128)S(1)}, f32[3,216,125]{2,1,0:T(8,128)}, u32[]{:S(2)}) copy-start(f32[3,216,125]{2,1,0:T(8,128)} %enrich_ref.1) | copy-start | bytes 972004
  27.7 0.9 %copy-start.6 = (bf16[216,192]{1,0:T(8,128)(2,1)S(1)}, bf16[216,192]{1,0:T(8,128)(2,1)}, u32[]{:S(2)}) copy-start(bf16[216,192]{1,0:T(8,128)(2,1)} %constant.13.clone.lift_ref) | copy-start | bytes 248836
  28.5 0.8 %copy-start.7 = (f32[5,5,256]{2,1,0:T(8,128)S(1)}, f32[5,5,256]{2,1,0:T(8,128)}, u32[]{:S(2)}) copy-start(f32[5,5,256]{2,1,0:T(8,128)} %jacobian_ref.1) | copy-start | bytes 76804
  29.3 0.8 %copy-start.8 = (bf16[64,216]{1,0:T(8,128)(2,1)S(1)}, bf16[64,216]{1,0:T(8,128)(2,1)}, u32[]{:S(2)}) copy-start(bf16[64,216]{1,0:T(8,128)(2,1)} %constant.14.clone.lift_edge_ref) | copy-start | bytes 82948
  30.1 0.7 %copy-start.10 = (s32[6,256]{1,0:T(8,128)S(1)}, s32[6,256]{1,0:T(8,128)}, u32[]{:S(2)}) copy-start(s32[6,256]{1,0:T(8,128)} %near_ref.1) | copy-start | bytes 18436
